TPU v7x, 128 devices: a whole 4x4x4 slice. The times are simulated.
128 devices in a mesh: row: 16 (over y_lo, x, core), col: 8 (over y_hi, z).
Axes of the slice: x: 4, y: 4 (y_hi: 2, y_lo: 2; y = y_hi * 2 + y_lo), z: 4, core: 2. Of those that a mesh axis runs over, the one named last changes fastest.
Arguments:
- resid: bfloat16 [2048, 5120], P('row', 'col'), may hold values from -160 to 160
- queries: bfloat16 [2048, 5120], P('row', 'col'), may hold values from -24 to 24
- keys: bfloat16 [2048, 5120], P('row', 'col'), may hold values from -24 to 24
- values: bfloat16 [2048, 5120], P('row', 'col'), may hold values from -6 to 6
- doc_ids: int32 [2048], replicated, may hold values from 0 to 7, never falling along the last dimension, each value on 1 to 1536 neighbouring positions
- norm_gain: float32 [5120], replicated, may hold values from 0.1 to 1.9
- expert_ids: int32 [2048, 6], P('row'), may hold values from 0 to 31, all different within a row; in each aligned block of 128 rows (0 to 127, 128 to 255, ...) at most 32 rows name the same one
- gate_levels: int32 [2048, 6], P('row'), may hold values from 1 to 64
- w_gate: bfloat16 [32, 1536, 5120], P('row', 'col'), may hold values from -0.078125 to 0.078125
- w_up: bfloat16 [32, 1536, 5120], P('row', 'col'), may hold values from -0.078125 to 0.078125
- w_down: bfloat16 [32, 1536, 5120], P('row', 'col'), may hold values from -0.15625 to 0.15625
- cotangent: bfloat16 [2048, 5120], P('row', 'col'), may hold values from -6 to 6
Outputs:
- d_normed: bfloat16 [2048, 5120], P('row', 'col')
- d_w_gate: bfloat16 [32, 1536, 5120], P('row', 'col')
- d_w_up: bfloat16 [32, 1536, 5120], P('row', 'col')
- d_w_down: bfloat16 [32, 1536, 5120], P('row', 'col')
Inputs may be any that keep to these rules, and one draw needn't show every extreme that they name: `doc_ids`: document numbers never fall along the tokens; one document spans exactly 1536 tokens. `expert_ids`: each token names 6 different experts. In each aligned block of 128 tokens (the tokens of one row index) no expert is named by more than 32 tokens, a bound that some block reaches.
All inputs are finite; a program needn't handle non-finite values.
Results may differ from a plain program's by a relative error of at most 0.017.
Values may be sent and summed in bfloat16 or wider, within the bound.
No kernel may reach another device: no remote copies, remote signals or barrier semaphores. Data moves between devices by JAX's collectives and lax.ppermute only.
A program may use at most 256 MiB of HBM per device.

v0:
```python
import math

import jax
import jax.numpy as jnp
from jax import lax
from jax.sharding import PartitionSpec as P

HEAD_DIM = 128
TOP = 6
WINDOW = 1024


def from_behind(x, axis, by):
    devices = lax.axis_size(axis)
    pairs = [(i, i + by) for i in range(devices) if 0 <= i + by < devices]
    return lax.ppermute(x, axis, pairs)


def body(
    resid,
    queries,
    keys,
    values,
    doc_ids,
    norm_gain,
    expert_ids,
    gate_levels,
    w_gate,
    w_up,
    w_down,
    cotangent,
):
    tok_rows, feat_width = queries.shape
    row_index = lax.axis_index("row")
    row_count = lax.axis_size("row")
    reach_count = WINDOW // tok_rows
    key_list = []
    value_list = []
    for distance in range(reach_count, 0, -1):
        moved_keys, moved_values = from_behind((keys, values), "row", distance)
        key_list.append(moved_keys)
        value_list.append(moved_values)
    all_keys = jnp.concatenate(key_list + [keys], axis=0)
    all_values = jnp.concatenate(value_list + [values], axis=0)
    key_total = (reach_count + 1) * tok_rows
    padded_docs = jnp.concatenate([jnp.full((reach_count * tok_rows,), -1, jnp.int32), doc_ids])
    key_docs = lax.dynamic_slice_in_dim(padded_docs, row_index * tok_rows, key_total)
    query_docs = lax.dynamic_slice_in_dim(doc_ids, row_index * tok_rows, tok_rows)
    query_pos = row_index * tok_rows + jnp.arange(tok_rows, dtype=jnp.int32)
    key_pos = (row_index - reach_count) * tok_rows + jnp.arange(key_total, dtype=jnp.int32)
    pos_delta = query_pos[:, None] - key_pos[None, :]
    allowed = (pos_delta >= 0) & (pos_delta < WINDOW) & (query_docs[:, None] == key_docs[None, :])
    heads_here = feat_width // HEAD_DIM
    query_heads = queries.reshape(tok_rows, heads_here, HEAD_DIM)
    key_heads = all_keys.reshape(key_total, heads_here, HEAD_DIM)
    value_heads = all_values.reshape(key_total, heads_here, HEAD_DIM)
    scores = jnp.einsum(
        "qhd,khd->hqk", query_heads, key_heads, preferred_element_type=jnp.float32
    ) * (1.0 / math.sqrt(HEAD_DIM))
    scores = jnp.where(allowed[None], scores, -1e30)
    top_score = jnp.max(scores, axis=2, keepdims=True)
    weights = jnp.exp(scores - top_score)
    probs = (weights / jnp.sum(weights, axis=2, keepdims=True)).astype(jnp.bfloat16)
    attention = jnp.einsum(
        "hqk,khd->qhd", probs, value_heads, preferred_element_type=jnp.float32
    ).reshape(tok_rows, feat_width)
    hidden_in = (resid.astype(jnp.float32) + attention).astype(jnp.bfloat16)
    local_experts = w_gate.shape[0]
    experts_total = local_experts * row_count
    capacity = 4 * tok_rows * TOP // (3 * experts_total)
    flat_ids = expert_ids.reshape(-1)
    matches = (flat_ids[:, None] == jnp.arange(experts_total, dtype=jnp.int32)[None, :]).astype(
        jnp.int32
    )
    slot_index = jnp.sum(matches * jnp.cumsum(matches, axis=0), axis=1) - 1
    target_index = flat_ids * capacity + slot_index
    assign_table = (
        jnp.full((experts_total * capacity,), tok_rows * TOP, jnp.int32)
        .at[target_index]
        .set(jnp.arange(tok_rows * TOP, dtype=jnp.int32))
    )
    token_table = assign_table // TOP
    gate_weights = gate_levels.reshape(-1).astype(jnp.float32) / 64.0
    full_hidden, full_grads = (
        lax.all_gather(hidden_in, "col", axis=1, tiled=True),
        lax.all_gather(cotangent, "col", axis=1, tiled=True),
    )
    widened = full_hidden.astype(jnp.float32)
    inv_rms = lax.rsqrt(jnp.mean(widened * widened, axis=1, keepdims=True) + 1e-05)
    normed = (widened * inv_rms * norm_gain[None, :]).astype(jnp.bfloat16)
    feat_count = normed.shape[1]
    zero_row = jnp.zeros((1, feat_count), jnp.bfloat16)
    scaled_grad = (
        gate_weights[:, None] * jnp.repeat(full_grads, TOP, axis=0).astype(jnp.float32)
    ).astype(jnp.bfloat16)
    routed_in = jnp.concatenate([normed, zero_row], axis=0)[token_table].reshape(
        row_count, local_experts, capacity, feat_count
    )
    routed_grad = jnp.concatenate([scaled_grad, zero_row], axis=0)[assign_table].reshape(
        row_count, local_experts, capacity, feat_count
    )
    recv_in, recv_grad = (
        lax.all_to_all(routed_in, "row", split_axis=0, concat_axis=0, tiled=True),
        lax.all_to_all(routed_grad, "row", split_axis=0, concat_axis=0, tiled=True),
    )
    pre_gate = jnp.einsum("secd,efd->secf", recv_in, w_gate, preferred_element_type=jnp.float32)
    pre_up = jnp.einsum("secd,efd->secf", recv_in, w_up, preferred_element_type=jnp.float32)
    gate_sigmoid = jax.nn.sigmoid(pre_gate)
    silu_gate = pre_gate * gate_sigmoid
    act = (silu_gate * pre_up).astype(jnp.bfloat16)
    grad_act = jnp.einsum("secd,efd->secf", recv_grad, w_down, preferred_element_type=jnp.float32)
    grad_gate = (grad_act * pre_up * gate_sigmoid * (1.0 + pre_gate * (1.0 - gate_sigmoid))).astype(
        jnp.bfloat16
    )
    grad_up = (grad_act * silu_gate).astype(jnp.bfloat16)
    d_w_down = jnp.einsum(
        "secf,secd->efd", act, recv_grad, preferred_element_type=jnp.float32
    ).astype(jnp.bfloat16)
    d_w_gate = jnp.einsum(
        "secf,secd->efd", grad_gate, recv_in, preferred_element_type=jnp.float32
    ).astype(jnp.bfloat16)
    d_w_up = jnp.einsum(
        "secf,secd->efd", grad_up, recv_in, preferred_element_type=jnp.float32
    ).astype(jnp.bfloat16)
    block_terms = jnp.einsum(
        "secf,efd->secd", grad_gate, w_gate, preferred_element_type=jnp.float32
    )
    block_terms = block_terms + jnp.einsum(
        "secf,efd->secd", grad_up, w_up, preferred_element_type=jnp.float32
    )
    block_terms = block_terms.astype(jnp.bfloat16)
    returned = lax.all_to_all(block_terms, "row", split_axis=0, concat_axis=0, tiled=True)
    flat_rows = returned.reshape(experts_total * capacity, -1)[target_index]
    d_normed = lax.psum_scatter(
        jnp.sum(flat_rows.astype(jnp.float32).reshape(tok_rows, TOP, -1), axis=1).astype(
            jnp.bfloat16
        ),
        "col",
        scatter_dimension=1,
        tiled=True,
    )
    return (d_normed, d_w_gate, d_w_up, d_w_down)


def solution(mesh):
    return jax.shard_map(
        body,
        mesh=mesh,
        in_specs=(
            P("row", "col"),
            P("row", "col"),
            P("row", "col"),
            P("row", "col"),
            P(),
            P(),
            P("row", None),
            P("row", None),
            P("row", "col", None),
            P("row", "col", None),
            P("row", "col", None),
            P("row", "col"),
        ),
        out_specs=(
            P("row", "col"),
            P("row", "col", None),
            P("row", "col", None),
            P("row", "col", None),
        ),
        check_vma=False,
    )
```

profile of v0, /device:TPU:0, one launch (start us, length us, event | category | flops | bytes accessed | tf_op | source)
XLA Modules:
  0.0 821.9 jit_solution(7680869357388876416)
XLA Ops:
  54.6 8.0 collective-permute-start.9
  104.5 48.0 %all-gather.5.cloned.1.call-done = bf16[128,5120]{1,0:T(8,128)(2,1)} async-done(((bf16[128,640]{1,0:T(8,128)(2,1)}), bf16[128,5120]{1,0:T(8,128)(2,1)}) %all-gather.5.cloned.1.call-update) | async-done | bytes 1310736 | tf_op jit(solution)/shard_map/all_gather | solution.py:85
  156.1 8.7 %gather_fusion.1 = bf16[1024,5120]{1,0:T(8,128)(2,1)} fusion(bf16[129,5120]{1,0:T(8,128)(2,1)S(1)} %concatenate.19, s32[1024]{0:T(1024)S(1)} %get-tuple-element.7), kind=kCustom, calls=%fused_computation.1 | custom fusion | bytes 20975616 | tf_op jit(solution)/shard_map/gather | solution.py:96
  169.8 13.7 %all-gather.3.cloned.1.call-start = ((), (), s32[]{:S(2)}) async-start(), calls=%async_computation.4 | async-start | bytes 1474560 | tf_op jit(solution)/shard_map/all_gather | solution.py:86
  183.8 110.6 %all-gather.3.cloned.1.call-done = bf16[128,5120]{1,0:T(8,128)(2,1)} async-done(((bf16[128,640]{1,0:T(8,128)(2,1)}), bf16[128,5120]{1,0:T(8,128)(2,1)}) %all-gather.3.cloned.1.call-update) | async-done | bytes 1310736 | tf_op jit(solution)/shard_map/all_gather | solution.py:86
  294.4 8.8 %broadcast_in_dim.20 = f32[128,6,5120]{2,1,0:T(8,128)} broadcast(bf16[128,5120]{1,0:T(8,128)(2,1)} %all-gather.3.cloned.1.call-done), dimensions={0,2} | broadcast | bytes 17039360 | tf_op jit(solution)/shard_map/broadcast_in_dim | solution.py:94
  303.2 18.4 %convert_element_type.67 = f32[768,5120]{1,0:T(8,128)} reshape(f32[128,6,5120]{2,1,0:T(8,128)} %broadcast_in_dim.20) | data formatting | bytes 31457280 | tf_op jit(solution)/shard_map/convert_element_type | solution.py:94
  331.8 22.8 %gather_fusion = bf16[1024,5120]{1,0:T(8,128)(2,1)} fusion(bf16[769,5120]{1,0:T(8,128)(2,1)} %concatenate.15, s32[1024]{0:T(1024)S(1)} %get-tuple-element.6), kind=kCustom, calls=%fused_computation | custom fusion | bytes 20975616 | tf_op jit(solution)/shard_map/gather | solution.py:99
  354.6 16.2 %all-to-all-start = ((bf16[16,2,32,5120]{3,2,1,0:T(8,128)(2,1)}), bf16[16,2,32,5120]{3,2,1,0:T(8,128)(2,1)}, u32[]{:S(2)}, u32[]{:S(2)}) async-start(bf16[16,2,32,5120]{3,2,1,0:T(8,128)(2,1)} %bitcast.96), calls=%async_computation | async-start | bytes 20971520 | tf_op jit(solution)/shard_map/all_to_all | solution.py:104
  370.8 6.9 fusion.33
  377.7 7.8 fusion.28
  385.6 126.2 %all-to-all-done = bf16[16,2,32,5120]{3,2,1,0:T(8,128)(2,1)} async-done(((bf16[16,2,32,5120]{3,2,1,0:T(8,128)(2,1)}), bf16[16,2,32,5120]{3,2,1,0:T(8,128)(2,1)}, u32[]{:S(2)}, u32[]{:S(2)}) %all-to-all-start) | async-done | bytes 10485792 | tf_op jit(solution)/shard_map/all_to_all | solution.py:104
  511.8 8.7 %multiply_convert_fusion.2 = (bf16[16,2,32,192]{3,2,0,1:T(8,128)(2,1)S(1)}, bf16[16,2,32,192]{3,2,0,1:T(8,128)(2,1)S(1)}) fusion(f32[16,2,32,192]{3,2,0,1:T(8,128)S(1)} %fusion.33, f32[16,2,32,192]{3,2,0,1:T(8,128)} %fusion.28, bf16[2,192,5120]{2,1,0:T(8,128)(2,1)} %param.22, bf16[16,2,32,5120]{3,2,1,0:T(8,128)(2,1)} %all-to-all-done), kind=kOutput, calls=%fused_computation.43 | convolution fusion | flops 2015821824 | bytes 16777216 | tf_op jit(solution)/shard_map/secd,efd->secf/dot_general | solution.py:111
  520.6 8.5 %fusion.15 = f32[2,16,32,5120]{3,2,1,0:T(8,128)} fusion(bf16[16,2,32,192]{3,2,0,1:T(8,128)(2,1)S(1)} %get-tuple-element.5, bf16[2,192,5120]{2,1,0:T(8,128)(2,1)S(1)} %copy-done), kind=kOutput, calls=%fused_computation.22 | convolution fusion | flops 2013265920 | bytes 25296896 | tf_op jit(solution)/shard_map/secf,efd->secd/dot_general | solution.py:125
  529.1 13.1 %fusion.5 = bf16[16,2,32,5120]{3,2,0,1:T(8,128)(2,1)} fusion(f32[2,16,32,5120]{3,2,1,0:T(8,128)} %fusion.15, bf16[16,2,32,192]{3,2,0,1:T(8,128)(2,1)S(1)} %get-tuple-element.4, bf16[2,192,5120]{2,1,0:T(8,128)(2,1)} %param.21), kind=kOutput, calls=%fused_computation.11 | convolution fusion | flops 2023751680 | bytes 35782656 | tf_op jit(solution)/shard_map/secf,efd->secd/dot_general | solution.py:128
  542.2 9.0 %copy.66 = bf16[16,2,32,5120]{3,2,1,0:T(8,128)(2,1)} copy(bf16[16,2,32,5120]{3,2,0,1:T(8,128)(2,1)} %fusion.5) | data formatting | bytes 20971520 | tf_op jit(solution)/shard_map/convert_element_type | solution.py:131
  556.1 8.2 bitcast_convert_fusion.1
  564.2 132.6 %all-to-all-done.2 = bf16[16,2,32,5120]{3,2,1,0:T(8,128)(2,1)} async-done(((bf16[16,2,32,5120]{3,2,1,0:T(8,128)(2,1)}), bf16[16,2,32,5120]{3,2,1,0:T(8,128)(2,1)}, u32[]{:S(2)}, u32[]{:S(2)}) %all-to-all-start.2) | async-done | bytes 10485792 | tf_op jit(solution)/shard_map/all_to_all | solution.py:132
  696.9 20.3 %gather_fusion.2 = bf16[768,5120]{1,0:T(8,128)(2,1)} fusion(bf16[1024,5120]{1,0:T(8,128)(2,1)} %bitcast.20, s32[1024]{0:T(1024)S(1)} %pad_clamp_fusion), kind=kCustom, calls=%fused_computation.2 | custom fusion | bytes 15731712 | tf_op jit(solution)/shard_map/gather | solution.py:133
  717.1 13.1 %gather.14 = bf16[128,6,5120]{2,1,0:T(8,128)(2,1)} reshape(bf16[768,5120]{1,0:T(8,128)(2,1)} %gather_fusion.2) | data formatting | bytes 15728640 | tf_op jit(solution)/shard_map/gather | solution.py:133
  730.2 10.4 %reduce_sum.42 = bf16[128,5120]{1,0:T(8,128)(2,1)S(1)} reduce(bf16[128,6,5120]{2,1,0:T(8,128)(2,1)} %gather.14, bf16[]{:T(256)} %constant.25.clone.1), dimensions={1}, to_apply=%region_7.8 | reduce | flops 3276800 | bytes 9175042 | tf_op jit(solution)/shard_map/reduce_sum | solution.py:135
  742.4 8.2 %bitcast_convert_fusion.2 = bf16[2,192,5120]{2,1,0:T(8,128)(2,1)} fusion(bf16[16,2,32,192]{3,2,0,1:T(8,128)(2,1)S(1)} %get-tuple-element.5, bf16[16,2,32,5120]{3,2,1,0:T(8,128)(2,1)} %all-to-all-done.1), kind=kOutput, calls=%fused_computation.14 | convolution fusion | flops 2015232000 | bytes 14811136 | tf_op jit(solution)/shard_map/secf,secd->efd/dot_general | solution.py:119
  750.6 8.4 %bitcast_convert_fusion = bf16[2,192,5120]{2,1,0:T(8,128)(2,1)} fusion(bf16[16,2,32,5120]{3,2,1,0:T(8,128)(2,1)} %all-to-all-done, f32[16,2,32,192]{3,2,0,1:T(8,128)S(1)} %copy-done.8, f32[16,2,32,192]{3,2,0,1:T(8,128)S(1)} %fusion.33), kind=kOutput, calls=%fused_computation.12 | convolution fusion | flops 2016411648 | bytes 15990784 | tf_op jit(solution)/shard_map/secf,secd->efd/dot_general | solution.py:116
  759.0 54.4 %reduce-scatter.4.cloned.1.call-done = bf16[640,128]{1,0:T(8,128)(2,1)} async-done(((bf16[5120,128]{1,0:T(8,128)(2,1)}), bf16[640,128]{1,0:T(8,128)(2,1)}) %reduce-scatter.4.cloned.1.call-update) | async-done | bytes 163856
  (114 shorter events, 116.1 us)
Async XLA Ops:
  7.2 60.0 %copy-start.3 = (bf16[128,640]{1,0:T(8,128)(2,1)S(1)}, bf16[128,640]{1,0:T(8,128)(2,1)}, u32[]{:S(2)}) copy-start(bf16[128,640]{1,0:T(8,128)(2,1)} %param.15) | copy-start | bytes 491524
  7.2 145.4 %all-gather.5.cloned.1.call-start = ((), (), s32[]{:S(2)}) async-start(), calls=%async_computation.5 | async-start | bytes 1474560 | tf_op jit(solution)/shard_map/all_gather | solution.py:85
  8.3 81.8 %collective-permute-start.15 = (bf16[128,640]{0,1:T(8,128)(2,1)S(1)}, bf16[128,640]{0,1:T(8,128)(2,1)S(1)}, u32[]{:S(2)}, u32[]{:S(2)}) collective-permute-start(bf16[128,640]{0,1:T(8,128)(2,1)S(1)} %copy.50), channel_id=1, source_target_pairs={{0,8},{8,16},{16,24},{24,32},{32,40},{40,48},{48,56},{56,64},{64,7... | collective-permute-start | bytes 491528 | tf_op jit(solution)/shard_map/ppermute | solution.py:16
  9.6 79.8 %collective-permute-start.14 = (bf16[128,640]{0,1:T(8,128)(2,1)S(1)}, bf16[128,640]{0,1:T(8,128)(2,1)S(1)}, u32[]{:S(2)}, u32[]{:S(2)}) collective-permute-start(bf16[128,640]{0,1:T(8,128)(2,1)S(1)} %copy.50), channel_id=1, source_target_pairs={{0,16},{8,24},{16,32},{24,40},{32,48},{40,56},{48,64},{56,72},{64,... | collective-permute-start | bytes 491528 | tf_op jit(solution)/shard_map/ppermute | solution.py:16
  13.7 74.1 %collective-permute-start.13 = (bf16[128,640]{0,1:T(8,128)(2,1)S(1)}, bf16[128,640]{0,1:T(8,128)(2,1)S(1)}, u32[]{:S(2)}, u32[]{:S(2)}) collective-permute-start(bf16[128,640]{0,1:T(8,128)(2,1)S(1)} %copy.50), channel_id=1, source_target_pairs={{0,24},{8,32},{16,40},{24,48},{32,56},{40,64},{48,72},{56,80},{64,... | collective-permute-start | bytes 491528 | tf_op jit(solution)/shard_map/ppermute | solution.py:16
  17.8 13.0 %collective-permute-start.1 = (bf16[128,640]{1,0:T(8,128)(2,1)}, bf16[128,640]{1,0:T(8,128)(2,1)S(1)}, u32[]{:S(2)}, u32[]{:S(2)}) collective-permute-start(bf16[128,640]{1,0:T(8,128)(2,1)} %param.15), channel_id=1, source_target_pairs={{0,56},{8,64},{16,72},{24,80},{32,88},{40,96},{48,104},{56,112},{6... | collective-permute-start | bytes 491528 | tf_op jit(solution)/shard_map/ppermute | solution.py:16
  22.5 7.0 collective-permute-start
  29.5 7.9 collective-permute-start.2
  30.8 11.1 %collective-permute-start.3 = (bf16[128,640]{1,0:T(8,128)(2,1)}, bf16[128,640]{1,0:T(8,128)(2,1)S(1)}, u32[]{:S(2)}, u32[]{:S(2)}) collective-permute-start(bf16[128,640]{1,0:T(8,128)(2,1)} %param.15), channel_id=1, source_target_pairs={{0,40},{8,48},{16,56},{24,64},{32,72},{40,80},{48,88},{56,96},{64,... | collective-permute-start | bytes 491528 | tf_op jit(solution)/shard_map/ppermute | solution.py:16
  37.4 8.5 %collective-permute-start.4 = (bf16[128,640]{1,0:T(8,128)(2,1)}, bf16[128,640]{1,0:T(8,128)(2,1)S(1)}, u32[]{:S(2)}, u32[]{:S(2)}) collective-permute-start(bf16[128,640]{1,0:T(8,128)(2,1)} %param.15), channel_id=1, source_target_pairs={{0,32},{8,40},{16,48},{24,56},{32,64},{40,72},{48,80},{56,88},{64,... | collective-permute-start | bytes 491528 | tf_op jit(solution)/shard_map/ppermute | solution.py:16
  41.9 8.4 %collective-permute-start.5 = (bf16[128,640]{1,0:T(8,128)(2,1)}, bf16[128,640]{1,0:T(8,128)(2,1)S(1)}, u32[]{:S(2)}, u32[]{:S(2)}) collective-permute-start(bf16[128,640]{1,0:T(8,128)(2,1)} %param.15), channel_id=1, source_target_pairs={{0,24},{8,32},{16,40},{24,48},{32,56},{40,64},{48,72},{56,80},{64,... | collective-permute-start | bytes 491528 | tf_op jit(solution)/shard_map/ppermute | solution.py:16
  46.0 8.6 %collective-permute-start.6 = (bf16[128,640]{1,0:T(8,128)(2,1)}, bf16[128,640]{1,0:T(8,128)(2,1)S(1)}, u32[]{:S(2)}, u32[]{:S(2)}) collective-permute-start(bf16[128,640]{1,0:T(8,128)(2,1)} %param.15), channel_id=1, source_target_pairs={{0,16},{8,24},{16,32},{24,40},{32,48},{40,56},{48,64},{56,72},{64,... | collective-permute-start | bytes 491528 | tf_op jit(solution)/shard_map/ppermute | solution.py:16
  50.3 12.3 %collective-permute-start.7 = (bf16[128,640]{1,0:T(8,128)(2,1)}, bf16[128,640]{1,0:T(8,128)(2,1)S(1)}, u32[]{:S(2)}, u32[]{:S(2)}) collective-permute-start(bf16[128,640]{1,0:T(8,128)(2,1)} %param.15), channel_id=1, source_target_pairs={{0,8},{8,16},{16,24},{24,32},{32,40},{40,48},{48,56},{56,64},{64,7... | collective-permute-start | bytes 491528 | tf_op jit(solution)/shard_map/ppermute | solution.py:16
  54.6 19.2 %collective-permute-start.9 = (bf16[128,640]{0,1:T(8,128)(2,1)S(1)}, bf16[128,640]{0,1:T(8,128)(2,1)S(1)}, u32[]{:S(2)}, u32[]{:S(2)}) collective-permute-start(bf16[128,640]{0,1:T(8,128)(2,1)S(1)} %copy.50), channel_id=1, source_target_pairs={{0,56},{8,64},{16,72},{24,80},{32,88},{40,96},{48,104},{56,112},{6... | collective-permute-start | bytes 491528 | tf_op jit(solution)/shard_map/ppermute | solution.py:16
  62.6 9.2 %collective-permute-start.8 = (bf16[128,640]{0,1:T(8,128)(2,1)S(1)}, bf16[128,640]{0,1:T(8,128)(2,1)S(1)}, u32[]{:S(2)}, u32[]{:S(2)}) collective-permute-start(bf16[128,640]{0,1:T(8,128)(2,1)S(1)} %copy.50), channel_id=1, source_target_pairs={{0,64},{8,72},{16,80},{24,88},{32,96},{40,104},{48,112},{56,120},{... | collective-permute-start | bytes 491528 | tf_op jit(solution)/shard_map/ppermute | solution.py:16
  71.8 7.7 collective-permute-start.10
  73.8 11.2 %collective-permute-start.11 = (bf16[128,640]{0,1:T(8,128)(2,1)S(1)}, bf16[128,640]{0,1:T(8,128)(2,1)S(1)}, u32[]{:S(2)}, u32[]{:S(2)}) collective-permute-start(bf16[128,640]{0,1:T(8,128)(2,1)S(1)} %copy.50), channel_id=1, source_target_pairs={{0,40},{8,48},{16,56},{24,64},{32,72},{40,80},{48,88},{56,96},{64,... | collective-permute-start | bytes 491528 | tf_op jit(solution)/shard_map/ppermute | solution.py:16
  79.5 7.7 collective-permute-start.12
  97.3 56.9 %copy-start.5 = (f32[5120]{0:T(1024)S(1)}, f32[5120]{0:T(1024)}, u32[]{:S(2)}) copy-start(f32[5120]{0:T(1024)} %param.17) | copy-start | bytes 61444
  164.8 189.8 %all-to-all-start.1 = ((bf16[16,2,32,5120]{3,2,1,0:T(8,128)(2,1)}), bf16[16,2,32,5120]{3,2,1,0:T(8,128)(2,1)}, u32[]{:S(2)}, u32[]{:S(2)}) async-start(bf16[16,2,32,5120]{3,2,1,0:T(8,128)(2,1)} %bitcast.95), calls=%async_computation.1 | async-start | bytes 20971520 | tf_op jit(solution)/shard_map/all_to_all | solution.py:103
  169.8 124.6 %all-gather.3.cloned.1.call-start = ((), (), s32[]{:S(2)}) async-start(), calls=%async_computation.4 | async-start | bytes 1474560 | tf_op jit(solution)/shard_map/all_gather | solution.py:86
  354.6 157.2 %all-to-all-start = ((bf16[16,2,32,5120]{3,2,1,0:T(8,128)(2,1)}), bf16[16,2,32,5120]{3,2,1,0:T(8,128)(2,1)}, u32[]{:S(2)}, u32[]{:S(2)}) async-start(bf16[16,2,32,5120]{3,2,1,0:T(8,128)(2,1)} %bitcast.96), calls=%async_computation | async-start | bytes 20971520 | tf_op jit(solution)/shard_map/all_to_all | solution.py:104
  551.2 145.7 %all-to-all-start.2 = ((bf16[16,2,32,5120]{3,2,1,0:T(8,128)(2,1)}), bf16[16,2,32,5120]{3,2,1,0:T(8,128)(2,1)}, u32[]{:S(2)}, u32[]{:S(2)}) async-start(bf16[16,2,32,5120]{3,2,1,0:T(8,128)(2,1)} %copy.66), calls=%async_computation.2 | async-start | bytes 20971520 | tf_op jit(solution)/shard_map/all_to_all | solution.py:132
  556.0 257.4 %reduce-scatter.4.cloned.1.call-start = ((), (), s32[]{:S(2)}) async-start(), calls=%async_computation.6 | async-start | bytes 1474560
  (7 other events, 52.7 us)
Sparse Core Ops, SparseCore 0:
  98.4 54.1 all-gather.4
  183.7 110.6 all-gather.2
  742.5 70.8 reduce-scatter.3
where the time goes:
time: 831 us; the launch traced here: 822 us
  waiting for transfers between devices  481 us (58%)
  local copies, waits for them, and re-layouts  124 us (15%)
  starting transfers between devices  102 us (12%)
  matrix products  75.7 us (9%)
  other arithmetic  25 us (3%)
  between operations  14.5 us (2%)
    all_to_all x1, waiting for transfers between devices, body(): lax.all_to_all(block_terms, 'row', split_axis=0, concat_axis=0, tiled=True)  133 us
    all_to_all x1, waiting for transfers between devices, body(): lax.all_to_all(routed_grad, 'row', split_axis=0, concat_axis=0, tiled=True)  126 us
    all_gather x1, waiting for transfers between devices, body(): lax.all_gather(cotangent, 'col', axis=1, tiled=True)  111 us
    ppermute x16, starting transfers between devices, from_behind(): return lax.ppermute(x, axis, pairs)  62.1 us
    unnamed x4, waiting for transfers between devices  54.4 us
    all_gather x1, waiting for transfers between devices, body(): lax.all_gather(hidden_in, 'col', axis=1, tiled=True)  48 us
    gather x2, local copies, waits for them, and re-layouts, body(): flat_rows = returned.reshape(experts_total * capacity, -1)[target_index]  33.4 us
    gather x1, local copies, waits for them, and re-layouts, body(): jnp.concatenate([scaled_grad, zero_row], axis=0)[assign_table]  22.8 us
  transfers between devices with their start and end apart: 22, of which 10 were waited for; matrix products, arithmetic and copies ran while one was open for 14% of the time, Pallas kernels for 0%

commit v1 on v0

--- a/solution.py
+++ b/solution.py
@@ -69,10 +69,9 @@
     experts_total = local_experts * row_count
     capacity = 4 * tok_rows * TOP // (3 * experts_total)
     flat_ids = expert_ids.reshape(-1)
-    matches = (flat_ids[:, None] == jnp.arange(experts_total, dtype=jnp.int32)[None, :]).astype(
-        jnp.int32
-    )
-    slot_index = jnp.sum(matches * jnp.cumsum(matches, axis=0), axis=1) - 1
+    order = jnp.arange(flat_ids.shape[0], dtype=jnp.int32)
+    earlier = (flat_ids[:, None] == flat_ids[None, :]) & (order[None, :] < order[:, None])
+    slot_index = jnp.sum(earlier.astype(jnp.int32), axis=1)
     target_index = flat_ids * capacity + slot_index
     assign_table = (
         jnp.full((experts_total * capacity,), tok_rows * TOP, jnp.int32)

time: 831 us -> 830 us (level)
  no operation moved by 1% of the time
where the time goes in v1:
time: 830 us; the launch traced here: 822 us
  waiting for transfers between devices  483 us (58%)
  local copies, waits for them, and re-layouts  123 us (15%)
  starting transfers between devices  102 us (12%)
  matrix products  75.7 us (9%)
  other arithmetic  23.5 us (3%)
  between operations  14.5 us (2%)
    all_to_all x1, waiting for transfers between devices, body(): lax.all_to_all(block_terms, 'row', split_axis=0, concat_axis=0, tiled=True)  133 us
    all_to_all x1, waiting for transfers between devices, body(): lax.all_to_all(routed_grad, 'row', split_axis=0, concat_axis=0, tiled=True)  126 us
    all_gather x1, waiting for transfers between devices, body(): lax.all_gather(cotangent, 'col', axis=1, tiled=True)  111 us
    ppermute x16, starting transfers between devices, from_behind(): return lax.ppermute(x, axis, pairs)  62.1 us
    unnamed x4, waiting for transfers between devices  54.4 us
    all_gather x1, waiting for transfers between devices, body(): lax.all_gather(hidden_in, 'col', axis=1, tiled=True)  50 us
    gather x2, local copies, waits for them, and re-layouts, body(): flat_rows = returned.reshape(experts_total * capacity, -1)[target_index]  33.4 us
    gather x1, local copies, waits for them, and re-layouts, body(): jnp.concatenate([scaled_grad, zero_row], axis=0)[assign_table]  22.8 us
  transfers between devices with their start and end apart: 22, of which 10 were waited for; matrix products, arithmetic and copies ran while one was open for 14% of the time, Pallas kernels for 0%

profile of v1, /device:TPU:0, one launch (start us, length us, event | category | flops | bytes accessed | tf_op | source)
XLA Modules:
  0.0 821.6 jit_solution(16630246079284193898)
XLA Ops:
  54.6 8.0 collective-permute-start.9
  102.6 50.0 %all-gather.5.cloned.1.call-done = bf16[128,5120]{1,0:T(8,128)(2,1)} async-done(((bf16[128,640]{1,0:T(8,128)(2,1)}), bf16[128,5120]{1,0:T(8,128)(2,1)}) %all-gather.5.cloned.1.call-update) | async-done | bytes 1310736 | tf_op jit(solution)/shard_map/all_gather | solution.py:84
  156.1 8.7 %gather_fusion.1 = bf16[1024,5120]{1,0:T(8,128)(2,1)} fusion(bf16[129,5120]{1,0:T(8,128)(2,1)S(1)} %concatenate.19, s32[1024]{0:T(1024)S(1)} %get-tuple-element.7), kind=kCustom, calls=%fused_computation.1 | custom fusion | bytes 20975616 | tf_op jit(solution)/shard_map/gather | solution.py:95
  169.8 13.7 %all-gather.3.cloned.1.call-start = ((), (), s32[]{:S(2)}) async-start(), calls=%async_computation.4 | async-start | bytes 1474560 | tf_op jit(solution)/shard_map/all_gather | solution.py:85
  183.8 110.5 %all-gather.3.cloned.1.call-done = bf16[128,5120]{1,0:T(8,128)(2,1)} async-done(((bf16[128,640]{1,0:T(8,128)(2,1)}), bf16[128,5120]{1,0:T(8,128)(2,1)}) %all-gather.3.cloned.1.call-update) | async-done | bytes 1310736 | tf_op jit(solution)/shard_map/all_gather | solution.py:85
  294.4 8.5 %broadcast_in_dim.20 = f32[128,6,5120]{2,1,0:T(8,128)} broadcast(bf16[128,5120]{1,0:T(8,128)(2,1)} %all-gather.3.cloned.1.call-done), dimensions={0,2} | broadcast | bytes 17039360 | tf_op jit(solution)/shard_map/broadcast_in_dim | solution.py:93
  302.9 18.4 %convert_element_type.65 = f32[768,5120]{1,0:T(8,128)} reshape(f32[128,6,5120]{2,1,0:T(8,128)} %broadcast_in_dim.20) | data formatting | bytes 31457280 | tf_op jit(solution)/shard_map/convert_element_type | solution.py:93
  331.4 22.8 %gather_fusion = bf16[1024,5120]{1,0:T(8,128)(2,1)} fusion(bf16[769,5120]{1,0:T(8,128)(2,1)} %concatenate.15, s32[1024]{0:T(1024)S(1)} %get-tuple-element.6), kind=kCustom, calls=%fused_computation | custom fusion | bytes 20975616 | tf_op jit(solution)/shard_map/gather | solution.py:98
  354.3 16.2 %all-to-all-start = ((bf16[16,2,32,5120]{3,2,1,0:T(8,128)(2,1)}), bf16[16,2,32,5120]{3,2,1,0:T(8,128)(2,1)}, u32[]{:S(2)}, u32[]{:S(2)}) async-start(bf16[16,2,32,5120]{3,2,1,0:T(8,128)(2,1)} %bitcast.80), calls=%async_computation | async-start | bytes 20971520 | tf_op jit(solution)/shard_map/all_to_all | solution.py:103
  370.5 6.9 fusion.34
  377.5 7.8 fusion.29
  385.3 126.2 %all-to-all-done = bf16[16,2,32,5120]{3,2,1,0:T(8,128)(2,1)} async-done(((bf16[16,2,32,5120]{3,2,1,0:T(8,128)(2,1)}), bf16[16,2,32,5120]{3,2,1,0:T(8,128)(2,1)}, u32[]{:S(2)}, u32[]{:S(2)}) %all-to-all-start) | async-done | bytes 10485792 | tf_op jit(solution)/shard_map/all_to_all | solution.py:103
  511.5 8.7 %multiply_convert_fusion.2 = (bf16[16,2,32,192]{3,2,0,1:T(8,128)(2,1)S(1)}, bf16[16,2,32,192]{3,2,0,1:T(8,128)(2,1)S(1)}) fusion(f32[16,2,32,192]{3,2,0,1:T(8,128)S(1)} %fusion.34, f32[16,2,32,192]{3,2,0,1:T(8,128)} %fusion.29, bf16[2,192,5120]{2,1,0:T(8,128)(2,1)} %param.22, bf16[16,2,32,5120]{3,2,1,0:T(8,128)(2,1)} %all-to-all-done), kind=kOutput, calls=%fused_computation.46 | convolution fusion | flops 2015821824 | bytes 16777216 | tf_op jit(solution)/shard_map/secd,efd->secf/dot_general | solution.py:110
  520.3 8.5 %fusion.15 = f32[2,16,32,5120]{3,2,1,0:T(8,128)} fusion(bf16[16,2,32,192]{3,2,0,1:T(8,128)(2,1)S(1)} %get-tuple-element.5, bf16[2,192,5120]{2,1,0:T(8,128)(2,1)S(1)} %copy-done), kind=kOutput, calls=%fused_computation.22 | convolution fusion | flops 2013265920 | bytes 25296896 | tf_op jit(solution)/shard_map/secf,efd->secd/dot_general | solution.py:124
  528.8 13.1 %fusion.5 = bf16[16,2,32,5120]{3,2,0,1:T(8,128)(2,1)} fusion(f32[2,16,32,5120]{3,2,1,0:T(8,128)} %fusion.15, bf16[16,2,32,192]{3,2,0,1:T(8,128)(2,1)S(1)} %get-tuple-element.4, bf16[2,192,5120]{2,1,0:T(8,128)(2,1)} %param.21), kind=kOutput, calls=%fused_computation.11 | convolution fusion | flops 2023751680 | bytes 35782656 | tf_op jit(solution)/shard_map/secf,efd->secd/dot_general | solution.py:127
  541.9 9.0 %copy.87 = bf16[16,2,32,5120]{3,2,1,0:T(8,128)(2,1)} copy(bf16[16,2,32,5120]{3,2,0,1:T(8,128)(2,1)} %fusion.5) | data formatting | bytes 20971520 | tf_op jit(solution)/shard_map/convert_element_type | solution.py:130
  555.8 8.2 bitcast_convert_fusion.1
  563.9 132.6 %all-to-all-done.2 = bf16[16,2,32,5120]{3,2,1,0:T(8,128)(2,1)} async-done(((bf16[16,2,32,5120]{3,2,1,0:T(8,128)(2,1)}), bf16[16,2,32,5120]{3,2,1,0:T(8,128)(2,1)}, u32[]{:S(2)}, u32[]{:S(2)}) %all-to-all-start.2) | async-done | bytes 10485792 | tf_op jit(solution)/shard_map/all_to_all | solution.py:131
  696.6 20.3 %gather_fusion.2 = bf16[768,5120]{1,0:T(8,128)(2,1)} fusion(bf16[1024,5120]{1,0:T(8,128)(2,1)} %bitcast.19, s32[1024]{0:T(1024)S(1)} %pad_clamp_fusion), kind=kCustom, calls=%fused_computation.2 | custom fusion | bytes 15731712 | tf_op jit(solution)/shard_map/gather | solution.py:132
  716.9 13.1 %gather.14 = bf16[128,6,5120]{2,1,0:T(8,128)(2,1)} reshape(bf16[768,5120]{1,0:T(8,128)(2,1)} %gather_fusion.2) | data formatting | bytes 15728640 | tf_op jit(solution)/shard_map/gather | solution.py:132
  730.0 10.4 %reduce_sum.45 = bf16[128,5120]{1,0:T(8,128)(2,1)S(1)} reduce(bf16[128,6,5120]{2,1,0:T(8,128)(2,1)} %gather.14, bf16[]{:T(256)} %constant.25.clone.1), dimensions={1}, to_apply=%region_5.6 | reduce | flops 3276800 | bytes 9175042 | tf_op jit(solution)/shard_map/reduce_sum | solution.py:134
  742.1 8.2 %bitcast_convert_fusion.2 = bf16[2,192,5120]{2,1,0:T(8,128)(2,1)} fusion(bf16[16,2,32,192]{3,2,0,1:T(8,128)(2,1)S(1)} %get-tuple-element.5, bf16[16,2,32,5120]{3,2,1,0:T(8,128)(2,1)} %all-to-all-done.1), kind=kOutput, calls=%fused_computation.14 | convolution fusion | flops 2015232000 | bytes 14811136 | tf_op jit(solution)/shard_map/secf,secd->efd/dot_general | solution.py:118
  750.4 8.4 %bitcast_convert_fusion = bf16[2,192,5120]{2,1,0:T(8,128)(2,1)} fusion(bf16[16,2,32,5120]{3,2,1,0:T(8,128)(2,1)} %all-to-all-done, f32[16,2,32,192]{3,2,0,1:T(8,128)S(1)} %copy-done.8, f32[16,2,32,192]{3,2,0,1:T(8,128)S(1)} %fusion.34), kind=kOutput, calls=%fused_computation.12 | convolution fusion | flops 2016411648 | bytes 15990784 | tf_op jit(solution)/shard_map/secf,secd->efd/dot_general | solution.py:115
  758.7 54.4 %reduce-scatter.4.cloned.1.call-done = bf16[640,128]{1,0:T(8,128)(2,1)} async-done(((bf16[5120,128]{1,0:T(8,128)(2,1)}), bf16[640,128]{1,0:T(8,128)(2,1)}) %reduce-scatter.4.cloned.1.call-update) | async-done | bytes 163856
  (108 shorter events, 114.2 us)
Async XLA Ops:
  7.2 60.0 %copy-start.3 = (bf16[128,640]{1,0:T(8,128)(2,1)S(1)}, bf16[128,640]{1,0:T(8,128)(2,1)}, u32[]{:S(2)}) copy-start(bf16[128,640]{1,0:T(8,128)(2,1)} %param.15) | copy-start | bytes 491524
  7.2 145.4 %all-gather.5.cloned.1.call-start = ((), (), s32[]{:S(2)}) async-start(), calls=%async_computation.5 | async-start | bytes 1474560 | tf_op jit(solution)/shard_map/all_gather | solution.py:84
  8.3 81.8 %collective-permute-start.15 = (bf16[128,640]{0,1:T(8,128)(2,1)S(1)}, bf16[128,640]{0,1:T(8,128)(2,1)S(1)}, u32[]{:S(2)}, u32[]{:S(2)}) collective-permute-start(bf16[128,640]{0,1:T(8,128)(2,1)S(1)} %copy.71), channel_id=1, source_target_pairs={{0,8},{8,16},{16,24},{24,32},{32,40},{40,48},{48,56},{56,64},{64,7... | collective-permute-start | bytes 491528 | tf_op jit(solution)/shard_map/ppermute | solution.py:16
  9.6 79.8 %collective-permute-start.14 = (bf16[128,640]{0,1:T(8,128)(2,1)S(1)}, bf16[128,640]{0,1:T(8,128)(2,1)S(1)}, u32[]{:S(2)}, u32[]{:S(2)}) collective-permute-start(bf16[128,640]{0,1:T(8,128)(2,1)S(1)} %copy.71), channel_id=1, source_target_pairs={{0,16},{8,24},{16,32},{24,40},{32,48},{40,56},{48,64},{56,72},{64,... | collective-permute-start | bytes 491528 | tf_op jit(solution)/shard_map/ppermute | solution.py:16
  13.7 74.1 %collective-permute-start.13 = (bf16[128,640]{0,1:T(8,128)(2,1)S(1)}, bf16[128,640]{0,1:T(8,128)(2,1)S(1)}, u32[]{:S(2)}, u32[]{:S(2)}) collective-permute-start(bf16[128,640]{0,1:T(8,128)(2,1)S(1)} %copy.71), channel_id=1, source_target_pairs={{0,24},{8,32},{16,40},{24,48},{32,56},{40,64},{48,72},{56,80},{64,... | collective-permute-start | bytes 491528 | tf_op jit(solution)/shard_map/ppermute | solution.py:16
  17.8 13.0 %collective-permute-start.1 = (bf16[128,640]{1,0:T(8,128)(2,1)}, bf16[128,640]{1,0:T(8,128)(2,1)S(1)}, u32[]{:S(2)}, u32[]{:S(2)}) collective-permute-start(bf16[128,640]{1,0:T(8,128)(2,1)} %param.15), channel_id=1, source_target_pairs={{0,56},{8,64},{16,72},{24,80},{32,88},{40,96},{48,104},{56,112},{6... | collective-permute-start | bytes 491528 | tf_op jit(solution)/shard_map/ppermute | solution.py:16
  22.5 7.0 collective-permute-start
  29.5 7.9 collective-permute-start.2
  30.8 11.1 %collective-permute-start.3 = (bf16[128,640]{1,0:T(8,128)(2,1)}, bf16[128,640]{1,0:T(8,128)(2,1)S(1)}, u32[]{:S(2)}, u32[]{:S(2)}) collective-permute-start(bf16[128,640]{1,0:T(8,128)(2,1)} %param.15), channel_id=1, source_target_pairs={{0,40},{8,48},{16,56},{24,64},{32,72},{40,80},{48,88},{56,96},{64,... | collective-permute-start | bytes 491528 | tf_op jit(solution)/shard_map/ppermute | solution.py:16
  37.4 8.5 %collective-permute-start.4 = (bf16[128,640]{1,0:T(8,128)(2,1)}, bf16[128,640]{1,0:T(8,128)(2,1)S(1)}, u32[]{:S(2)}, u32[]{:S(2)}) collective-permute-start(bf16[128,640]{1,0:T(8,128)(2,1)} %param.15), channel_id=1, source_target_pairs={{0,32},{8,40},{16,48},{24,56},{32,64},{40,72},{48,80},{56,88},{64,... | collective-permute-start | bytes 491528 | tf_op jit(solution)/shard_map/ppermute | solution.py:16
  41.9 8.4 %collective-permute-start.5 = (bf16[128,640]{1,0:T(8,128)(2,1)}, bf16[128,640]{1,0:T(8,128)(2,1)S(1)}, u32[]{:S(2)}, u32[]{:S(2)}) collective-permute-start(bf16[128,640]{1,0:T(8,128)(2,1)} %param.15), channel_id=1, source_target_pairs={{0,24},{8,32},{16,40},{24,48},{32,56},{40,64},{48,72},{56,80},{64,... | collective-permute-start | bytes 491528 | tf_op jit(solution)/shard_map/ppermute | solution.py:16
  46.0 8.6 %collective-permute-start.6 = (bf16[128,640]{1,0:T(8,128)(2,1)}, bf16[128,640]{1,0:T(8,128)(2,1)S(1)}, u32[]{:S(2)}, u32[]{:S(2)}) collective-permute-start(bf16[128,640]{1,0:T(8,128)(2,1)} %param.15), channel_id=1, source_target_pairs={{0,16},{8,24},{16,32},{24,40},{32,48},{40,56},{48,64},{56,72},{64,... | collective-permute-start | bytes 491528 | tf_op jit(solution)/shard_map/ppermute | solution.py:16
  50.3 12.3 %collective-permute-start.7 = (bf16[128,640]{1,0:T(8,128)(2,1)}, bf16[128,640]{1,0:T(8,128)(2,1)S(1)}, u32[]{:S(2)}, u32[]{:S(2)}) collective-permute-start(bf16[128,640]{1,0:T(8,128)(2,1)} %param.15), channel_id=1, source_target_pairs={{0,8},{8,16},{16,24},{24,32},{32,40},{40,48},{48,56},{56,64},{64,7... | collective-permute-start | bytes 491528 | tf_op jit(solution)/shard_map/ppermute | solution.py:16
  54.6 19.2 %collective-permute-start.9 = (bf16[128,640]{0,1:T(8,128)(2,1)S(1)}, bf16[128,640]{0,1:T(8,128)(2,1)S(1)}, u32[]{:S(2)}, u32[]{:S(2)}) collective-permute-start(bf16[128,640]{0,1:T(8,128)(2,1)S(1)} %copy.71), channel_id=1, source_target_pairs={{0,56},{8,64},{16,72},{24,80},{32,88},{40,96},{48,104},{56,112},{6... | collective-permute-start | bytes 491528 | tf_op jit(solution)/shard_map/ppermute | solution.py:16
  62.6 9.2 %collective-permute-start.8 = (bf16[128,640]{0,1:T(8,128)(2,1)S(1)}, bf16[128,640]{0,1:T(8,128)(2,1)S(1)}, u32[]{:S(2)}, u32[]{:S(2)}) collective-permute-start(bf16[128,640]{0,1:T(8,128)(2,1)S(1)} %copy.71), channel_id=1, source_target_pairs={{0,64},{8,72},{16,80},{24,88},{32,96},{40,104},{48,112},{56,120},{... | collective-permute-start | bytes 491528 | tf_op jit(solution)/shard_map/ppermute | solution.py:16
  71.8 7.7 collective-permute-start.10
  73.8 11.2 %collective-permute-start.11 = (bf16[128,640]{0,1:T(8,128)(2,1)S(1)}, bf16[128,640]{0,1:T(8,128)(2,1)S(1)}, u32[]{:S(2)}, u32[]{:S(2)}) collective-permute-start(bf16[128,640]{0,1:T(8,128)(2,1)S(1)} %copy.71), channel_id=1, source_target_pairs={{0,40},{8,48},{16,56},{24,64},{32,72},{40,80},{48,88},{56,96},{64,... | collective-permute-start | bytes 491528 | tf_op jit(solution)/shard_map/ppermute | solution.py:16
  79.5 7.7 collective-permute-start.12
  97.3 56.9 %copy-start.5 = (f32[5120]{0:T(1024)S(1)}, f32[5120]{0:T(1024)}, u32[]{:S(2)}) copy-start(f32[5120]{0:T(1024)} %param.17) | copy-start | bytes 61444
  164.8 189.5 %all-to-all-start.1 = ((bf16[16,2,32,5120]{3,2,1,0:T(8,128)(2,1)}), bf16[16,2,32,5120]{3,2,1,0:T(8,128)(2,1)}, u32[]{:S(2)}, u32[]{:S(2)}) async-start(bf16[16,2,32,5120]{3,2,1,0:T(8,128)(2,1)} %bitcast.79), calls=%async_computation.1 | async-start | bytes 20971520 | tf_op jit(solution)/shard_map/all_to_all | solution.py:102
  169.8 124.6 %all-gather.3.cloned.1.call-start = ((), (), s32[]{:S(2)}) async-start(), calls=%async_computation.4 | async-start | bytes 1474560 | tf_op jit(solution)/shard_map/all_gather | solution.py:85
  354.3 157.2 %all-to-all-start = ((bf16[16,2,32,5120]{3,2,1,0:T(8,128)(2,1)}), bf16[16,2,32,5120]{3,2,1,0:T(8,128)(2,1)}, u32[]{:S(2)}, u32[]{:S(2)}) async-start(bf16[16,2,32,5120]{3,2,1,0:T(8,128)(2,1)} %bitcast.80), calls=%async_computation | async-start | bytes 20971520 | tf_op jit(solution)/shard_map/all_to_all | solution.py:103
  550.9 145.7 %all-to-all-start.2 = ((bf16[16,2,32,5120]{3,2,1,0:T(8,128)(2,1)}), bf16[16,2,32,5120]{3,2,1,0:T(8,128)(2,1)}, u32[]{:S(2)}, u32[]{:S(2)}) async-start(bf16[16,2,32,5120]{3,2,1,0:T(8,128)(2,1)} %copy.87), calls=%async_computation.2 | async-start | bytes 20971520 | tf_op jit(solution)/shard_map/all_to_all | solution.py:131
  555.7 257.4 %reduce-scatter.4.cloned.1.call-start = ((), (), s32[]{:S(2)}) async-start(), calls=%async_computation.6 | async-start | bytes 1474560
  (7 other events, 52.7 us)
Sparse Core Ops, SparseCore 0:
  98.4 54.1 all-gather.4
  183.7 110.6 all-gather.2
  742.2 70.8 reduce-scatter.3

commit v2 on v1

v2 whole, which is shorter than its diff:
```python
import math

import jax
import jax.numpy as jnp
from jax import lax
from jax.experimental import pallas as pl
from jax.experimental.pallas import tpu as pltpu
from jax.sharding import PartitionSpec as P

HEAD_DIM = 128
WINDOW = 1024
EPS = 1e-05
VMEM = 56 * 2**20
F32, BF16 = jnp.float32, jnp.bfloat16
CORE = 8


def mask_x(k):
    return k << 4


def mask_z(k):
    return k


def mask_y(k):
    return ((k >> 1) << 2) | ((k & 1) << 6)


def swap(x, mask):
    return lax.ppermute(x, ("row", "col"), [(i, i ^ mask) for i in range(128)])


def gather_direct(x, mask):
    return jnp.stack([x, swap(x, mask(1)), swap(x, mask(2)), swap(x, mask(3))])


def gather_ring(x, mask):
    half = x.shape[0] // 2
    one, three = swap(x, mask(1)), swap(x, mask(3))
    low, high = swap(three[:half], mask(1)), swap(one[half:], mask(3))
    return jnp.concatenate([x, one, low, high, three]).reshape(4, *x.shape)


def add(*terms):
    return sum(t.astype(F32) for t in terms).astype(BF16)


def scatter_ring(p, mask):
    half = p.shape[1] // 2
    from_one, from_three = swap(p[2, :half], mask(1)), swap(p[2, half:], mask(3))
    for_one = jnp.concatenate([p[1, :half], add(p[1, half:], from_three)])
    for_three = jnp.concatenate([add(p[3, :half], from_one), p[3, half:]])
    return add(p[0], swap(for_one, mask(1)), swap(for_three, mask(3)))


def scatter_direct(p, mask):
    return add(p[0], swap(p[1], mask(1)), swap(p[2], mask(2)), swap(p[3], mask(3)))


ORDERS = ((mask_z, mask_y, mask_x), (mask_x, mask_z, mask_y), (mask_y, mask_x, mask_z))


def split_rows(rows):
    step = rows // 8
    return ((0, 3 * step), (3 * step, 3 * step), (6 * step, 2 * step))


def gather_tokens(x):
    parts = []
    for (start, size), (first, second, last) in zip(split_rows(x.shape[0]), ORDERS):
        part = gather_direct(x[start : start + size], first)
        part = gather_direct(part, second)
        parts.append(gather_ring(part, last))
    a, b, c = parts
    r, w = x.shape[0], x.shape[1]
    return (
        a.reshape(4, 2, 2, 4, -1, w),
        b.reshape(2, 2, 4, 4, -1, w),
        c.reshape(4, 4, 2, 2, -1, w),
    )


def scatter_tokens(parts):
    outs = []
    for part, (first, second, last) in zip(parts, ORDERS):
        part = part.reshape(4, 4, 4, *part.shape[-2:])
        part = scatter_ring(part, last)
        part = scatter_direct(part, second)
        outs.append(scatter_direct(part, first))
    return jnp.concatenate(outs)


def part_specs(sizes, width):
    a, b, c = sizes
    return [
        pl.BlockSpec((4, None, 2, None, a, width), lambda f, s: (0, f // 4, 0, f % 4, 0, 0)),
        pl.BlockSpec((None, 2, None, 4, b, width), lambda f, s: (f // 4, 0, f % 4, 0, 0, 0)),
        pl.BlockSpec((None, 4, None, 2, c, width), lambda f, s: (f % 4, 0, f // 4, 0, 0, 0)),
    ]


def part_shapes(sizes, width):
    a, b, c = sizes
    return [
        jax.ShapeDtypeStruct((4, 2, 2, 4, a, width), BF16),
        jax.ShapeDtypeStruct((2, 2, 4, 4, b, width), BF16),
        jax.ShapeDtypeStruct((4, 4, 2, 2, c, width), BF16),
    ]


def rows_of(ref):
    return ref[...].reshape(-1, ref.shape[-1])


def dot_nt(a, b):
    return lax.dot_general(a, b, (((1,), (1,)), ((), ())), preferred_element_type=F32)


def dot_nn(a, b):
    return lax.dot_general(a, b, (((1,), (0,)), ((), ())), preferred_element_type=F32)


def weight_spec(w, width):
    return pl.BlockSpec((w.shape[0], w.shape[1], width), lambda f, s: (0, 0, f ^ s[0]))


def whole(shape):
    return pl.BlockSpec(shape, lambda f, s: (0,) * len(shape))


def call(kernel, col, steps, in_specs, out_specs, out_shape, scratch, args, flops, moved):
    return pl.pallas_call(
        kernel,
        out_shape=out_shape,
        grid_spec=pltpu.PrefetchScalarGridSpec(
            num_scalar_prefetch=1,
            grid=(steps,),
            in_specs=in_specs,
            out_specs=out_specs,
            scratch_shapes=scratch,
        ),
        compiler_params=pltpu.CompilerParams(vmem_limit_bytes=VMEM),
        cost_estimate=pl.CostEstimate(flops=flops, bytes_accessed=moved, transcendentals=0),
    )(col, *args)


def attention_kernel(q, own, sib, resid, qdoc, kdoc, qpos, kpos, out):
    width = q.shape[1]
    keys = own.shape[0]
    delta = qpos[...] - kpos[...]
    allowed = (delta >= 0) & (delta < WINDOW) & (qdoc[...] == kdoc[...])
    for h in range(width // HEAD_DIM):
        cols = slice(h * HEAD_DIM, (h + 1) * HEAD_DIM)
        vcols = slice(width + h * HEAD_DIM, width + (h + 1) * HEAD_DIM)
        s = jnp.concatenate([dot_nt(q[:, cols], own[:, cols]), dot_nt(q[:, cols], sib[:, cols])], axis=1)
        s = jnp.where(allowed, s * (1.0 / math.sqrt(HEAD_DIM)), -1e30)
        e = jnp.exp(s - jnp.max(s, axis=1, keepdims=True))
        p = (e / jnp.sum(e, axis=1, keepdims=True)).astype(BF16)
        o = dot_nn(p[:, :keys], own[:, vcols]) + dot_nn(p[:, keys:], sib[:, vcols])
        out[:, cols] = (resid[:, cols].astype(F32) + o).astype(BF16)


def attend(queries, keys, values, resid, doc_ids, row):
    rows, width = queries.shape
    reach = WINDOW // rows
    pair = jnp.concatenate([keys, values], axis=1)
    blocks = []
    for by in range(reach, 0, -2):
        blocks.append(lax.ppermute(pair, "row", [(i, i + by) for i in range(16 - by)]))
    own = jnp.concatenate(blocks + [pair])
    sib = swap(own, CORE)
    padded = jnp.concatenate([jnp.full(((reach + 1) * rows,), -1, jnp.int32), doc_ids])

    def info(r):
        first = r - reach
        docs = lax.dynamic_slice_in_dim(padded, (first + reach + 1) * rows, (reach + 1) * rows)
        pos = first * rows + jnp.arange((reach + 1) * rows, dtype=jnp.int32)
        return docs.reshape(reach + 1, rows)[::2].reshape(1, -1), pos.reshape(reach + 1, rows)[::2].reshape(1, -1)

    (d0, p0), (d1, p1) = info(row), info(row ^ 1)
    kdoc, kpos = jnp.concatenate([d0, d1], axis=1), jnp.concatenate([p0, p1], axis=1)
    kdoc = jnp.where(kpos >= 0, kdoc, -1)
    qdoc = lax.dynamic_slice_in_dim(doc_ids, row * rows, rows)[:, None]
    qpos = row * rows + jnp.arange(rows, dtype=jnp.int32)[:, None]
    return pl.pallas_call(
        attention_kernel,
        out_shape=jax.ShapeDtypeStruct((rows, width), BF16),
        compiler_params=pltpu.CompilerParams(vmem_limit_bytes=VMEM),
        cost_estimate=pl.CostEstimate(flops=4 * rows * width * own.shape[0] * 2, bytes_accessed=4 * own.size, transcendentals=0),
    )(queries, own, sib, resid, qdoc, kdoc, qpos, kpos)


def grad_act_kernel(s, xa, xb, xc, w0, w1, out):
    @pl.when(pl.program_id(0) == 0)
    def _():
        out[...] = jnp.zeros_like(out)

    n = out.shape[1] // 2
    start = 0
    for x in (xa, xb, xc):
        x = rows_of(x)
        span = slice(start, start + x.shape[0])
        start += x.shape[0]
        out[span, :n] += dot_nt(x, rows_of(w0))
        out[span, n:] += dot_nt(x, rows_of(w1))


def hidden_kernel(
    s, xa, xb, xc, wg0, wg1, wu0, wu1, gain, gact, gates, gg_out, gu_out, act_t, gg_t, gu_t, g_acc, u_acc, sq_acc
):
    f = pl.program_id(0)
    tokens, hidden = g_acc.shape
    n = hidden // 2

    @pl.when(f == 0)
    def _():
        g_acc[...] = jnp.zeros_like(g_acc)
        u_acc[...] = jnp.zeros_like(u_acc)
        sq_acc[...] = jnp.zeros_like(sq_acc)

    start = 0
    for x in (xa, xb, xc):
        x = rows_of(x).astype(F32)
        span = slice(start, start + x.shape[0])
        start += x.shape[0]
        sq = x * x
        total = sq[:, :128]
        for j in range(128, x.shape[1], 128):
            total += sq[:, j : j + 128]
        sq_acc[span] += total
        x = (x * gain[...]).astype(BF16)
        g_acc[span, :n] += dot_nt(x, rows_of(wg0))
        g_acc[span, n:] += dot_nt(x, rows_of(wg1))
        u_acc[span, :n] += dot_nt(x, rows_of(wu0))
        u_acc[span, n:] += dot_nt(x, rows_of(wu1))

    @pl.when(f == pl.num_programs(0) - 1)
    def _():
        feats = pl.num_programs(0) * xa.shape[-1]
        expert = lax.broadcasted_iota(jnp.int32, (1, hidden), 1) // (hidden // 4)
        for r in range(0, tokens, 128):
            span = slice(r, r + 128)
            inv = lax.rsqrt(jnp.sum(sq_acc[span], axis=1, keepdims=True) * (1.0 / feats) + EPS)
            gate = jnp.where(
                expert < 2,
                jnp.where(expert == 0, gates[span, 0:1], gates[span, 1:2]),
                jnp.where(expert == 2, gates[span, 2:3], gates[span, 3:4]),
            )
            pre_gate, pre_up = g_acc[span] * inv, u_acc[span] * inv
            sig = jax.nn.sigmoid(pre_gate)
            silu = pre_gate * sig
            grad = gact[span] * gate
            gg = grad * pre_up * sig * (1.0 + pre_gate * (1.0 - sig))
            gu = grad * silu
            gg_out[span] = gg.astype(BF16)
            gu_out[span] = gu.astype(BF16)
            act_t[:, span] = (silu * pre_up * gate).T.astype(BF16)
            gg_t[:, span] = (gg * inv).T.astype(BF16)
            gu_t[:, span] = (gu * inv).T.astype(BF16)


def piece_kernel(s, gg, gu, wg0, wg1, wu0, wu1, oa, ob, oc):
    n = gg.shape[1] // 2
    start = 0
    for o in (oa, ob, oc):
        size = o.shape[0] * o.shape[1] * o.shape[2]
        span = slice(start, start + size)
        start += size
        out = dot_nn(gg[span, :n], rows_of(wg0)) + dot_nn(gg[span, n:], rows_of(wg1))
        out += dot_nn(gu[span, :n], rows_of(wu0)) + dot_nn(gu[span, n:], rows_of(wu1))
        o[...] = out.astype(BF16).reshape(o.shape)


def weight_grad_kernel(with_more, s, gain, *refs):
    xs, cs = refs[:3], refs[3:6]
    act_t, gg_t, gu_t = refs[6:9]
    more = refs[9:12] if with_more else (None,) * 3
    dg, du, dd = refs[-3:]
    for lhs, data, scale, extra, out in (
        (gg_t, xs, gain, more[0], dg),
        (gu_t, xs, gain, more[1], du),
        (act_t, cs, None, more[2], dd),
    ):
        start = 0
        total = None
        for x in data:
            x = rows_of(x)
            term = dot_nn(lhs[:, start : start + x.shape[0]], x)
            start += x.shape[0]
            total = term if total is None else total + term
        if scale is not None:
            total = total * scale[...]
        if extra is not None:
            total = total + rows_of(extra).astype(F32)
        out[...] = total.astype(BF16).reshape(out.shape)


def body(
    resid, queries, keys, values, doc_ids, norm_gain, expert_ids, gate_levels, w_gate, w_up, w_down, cotangent
):
    rows, width = queries.shape
    row, col = lax.axis_index("row"), lax.axis_index("col")
    experts, inner, feats = w_gate.shape
    steps = feats // width
    hidden = 2 * experts * inner
    tokens = 8 * rows
    sizes = [size for _, size in split_rows(rows)]
    here = jnp.reshape(col, (1,)).astype(jnp.int32)

    hidden_in = attend(queries, keys, values, resid, doc_ids, row)
    ids = jnp.arange(16 * experts, dtype=jnp.int32)
    table = jnp.sum(
        jnp.where(expert_ids[:, :, None] == ids, gate_levels[:, :, None].astype(F32) / 64.0, 0.0), axis=1
    ).astype(BF16)
    table = gather_direct(table, mask_x)
    table = jnp.stack([table, swap(table, mask_y(1))])
    gates = []
    for (start, size), swapped in zip(split_rows(rows), (True, False, True)):
        part = table[:, :, start : start + size]
        gates.append((jnp.swapaxes(part, 0, 1) if swapped else part).reshape(8 * size, -1))
    gates = jnp.concatenate(gates)
    gates = jnp.concatenate(
        [lax.dynamic_slice_in_dim(gates, experts * r, experts, axis=1) for r in (row, row ^ 1)], axis=1
    ).astype(F32)

    sib_down, sib_gate, sib_up = swap(w_down, CORE), swap(w_gate, CORE), swap(w_up, CORE)
    cot = gather_tokens(cotangent)
    x = gather_tokens(hidden_in)
    gain = norm_gain.reshape(1, feats)

    xs = part_specs(sizes, width)
    ws = weight_spec(w_gate, width)
    gain_spec = pl.BlockSpec((1, width), lambda f, s: (0, f ^ s[0]))
    one = 2 * tokens * hidden * feats
    grad_act = call(
        grad_act_kernel, here, steps, xs + [ws] * 2, whole((tokens, hidden)),
        jax.ShapeDtypeStruct((tokens, hidden), F32), [], (*cot, w_down, sib_down), one, 2 * tokens * feats * 2,
    )
    flat = jax.ShapeDtypeStruct((tokens, hidden), BF16)
    turned = jax.ShapeDtypeStruct((hidden, tokens), BF16)
    gg, gu, act_t, gg_t, gu_t = call(
        hidden_kernel, here, steps,
        xs + [ws] * 4 + [gain_spec, whole((tokens, hidden)), whole((tokens, 4))],
        [whole((tokens, hidden))] * 2 + [whole((hidden, tokens))] * 3,
        [flat, flat, turned, turned, turned],
        [pltpu.VMEM((tokens, hidden), F32), pltpu.VMEM((tokens, hidden), F32), pltpu.VMEM((tokens, 128), F32)],
        (*x, w_gate, sib_gate, w_up, sib_up, gain, grad_act, gates), 2 * one, 4 * tokens * feats,
    )
    pieces = call(
        piece_kernel, here, steps, [whole((tokens, hidden))] * 2 + [ws] * 4, xs, part_shapes(sizes, width), [],
        (gg, gu, w_gate, sib_gate, w_up, sib_up), 2 * one, 4 * tokens * feats,
    )
    d_normed = scatter_tokens(pieces)

    def weight_grads(which, more):
        half = pl.BlockSpec((hidden // 2, tokens), lambda f, s: (which, 0))
        return call(
            lambda *refs: weight_grad_kernel(bool(more), *refs), here, steps,
            [gain_spec] + xs * 2 + [half] * 3 + [ws] * len(more), [ws] * 3,
            [jax.ShapeDtypeStruct(w_gate.shape, BF16)] * 3, [],
            (gain, *x, *cot, act_t, gg_t, gu_t, *more), 3 * one // 2, 4 * tokens * feats,
        )

    sent = weight_grads(1, ())
    d_gate, d_up, d_down = weight_grads(0, tuple(swap(d, CORE) for d in sent))
    return (d_normed, d_gate, d_up, d_down)


def solution(mesh):
    tile, split3 = P("row", "col"), P("row", "col", None)
    return jax.shard_map(
        body,
        mesh=mesh,
        in_specs=(tile, tile, tile, tile, P(), P(), P("row", None), P("row", None), split3, split3, split3, tile),
        out_specs=(tile, split3, split3, split3),
        check_vma=False,
    )
```

time: 830 us -> 527 us (0.63)
  waiting for transfers between devices: 483 us -> 181 us
  Pallas kernels: 0 us -> 139 us
  local copies, waits for them, and re-layouts: 123 us -> 25.5 us
  matrix products: 75.7 us -> 0 us
  starting transfers between devices: 102 us -> 153 us
  between operations: 14.5 us -> 2.28 us
    all_to_all x3 -> x0, waiting for transfers between devices: 259 us -> none  [the longest x1 133 us: body(): lax.all_to_all(block_terms, 'row', split_axis=0, concat_axis=0, tiled=True)]
    ppermute x16 -> x105, waiting for transfers between devices: 8.88 us -> 181 us  [the longest x101 181 us: swap(): return lax.ppermute(x, ('row', 'col'), [(i, i ^ mask) for i in range(128)])]
    all_gather x2 -> x0, waiting for transfers between devices: 161 us -> none  [the longest x1 111 us: body(): lax.all_gather(cotangent, 'col', axis=1, tiled=True)]
    pallas_call x0 -> x6, Pallas kernels: none -> 139 us  [the longest x5 133 us: call(): pl.pallas_call(kernel, out_shape=out_shape, grid_spec=pltpu.PrefetchScala...]
    ppermute x16 -> x105, starting transfers between devices: 62.1 us -> 153 us  [the longest x101 141 us: swap(): return lax.ppermute(x, ('row', 'col'), [(i, i ^ mask) for i in range(128)])]
    dot_general x9 -> x0, matrix products: 72.9 us -> none  [the longest x1 13.1 us: body(): jnp.einsum('secf,efd->secd', grad_up, w_up, preferred_element_type=jnp.fl...]
    gather x4 -> x0, local copies, waits for them, and re-layouts: 65 us -> none  [the longest x2 33.4 us: body(): flat_rows = returned.reshape(experts_total * capacity, -1)[target_index]]
    unnamed x4 -> x0, waiting for transfers between devices: 54.4 us -> none
  transfers between devices with their start and end apart: 22 -> 105, of which waited for: 10 -> 44; matrix products, arithmetic and copies ran while one was open for 14% -> 6% of each run, Pallas kernels for 0% -> 8%
where the time goes in v2:
time: 527 us; the launch traced here: 518 us
  waiting for transfers between devices  181 us (34%)
  starting transfers between devices  153 us (29%)
  Pallas kernels  139 us (26%)
  local copies, waits for them, and re-layouts  25.5 us (5%)
  other arithmetic  17.5 us (3%)
    ppermute x101, waiting for transfers between devices, swap(): return lax.ppermute(x, ('row', 'col'), [(i, i ^ mask) for i in range(128)])  181 us
    ppermute x101, starting transfers between devices, swap(): return lax.ppermute(x, ('row', 'col'), [(i, i ^ mask) for i in range(128)])  141 us
    pallas_call x5, Pallas kernels, call(): pl.pallas_call(kernel, out_shape=out_shape, grid_spec=pltpu.PrefetchScala...  133 us
    ppermute x4, starting transfers between devices, attend(): lax.ppermute(pair, 'row', [(i, i + by) for i in range(16 - by)])  12.4 us
  transfers between devices with their start and end apart: 105, of which 44 were waited for; matrix products, arithmetic and copies ran while one was open for 6% of the time, Pallas kernels for 8%

profile of v2, /device:TPU:0, one launch (start us, length us, event | category | flops | bytes accessed | tf_op | source)
XLA Modules:
  0.0 518.1 jit_solution(7080914370626368487)
XLA Ops:
  31.5 4.9 collective-permute-start.2
  43.4 12.3 %collective-permute-done.60 = bf16[4,32,640]{2,1,0:T(8,128)(2,1)S(1)} collective-permute-done((bf16[4,32,640]{2,1,0:T(8,128)(2,1)S(1)}, bf16[4,32,640]{2,1,0:T(8,128)(2,1)S(1)}, u32[]{:S(2)}, u32[]{:S(2)}) %collective-permute-start.60) | collective-permute-done | bytes 163872 | tf_op jit(solution)/shard_map/ppermute | solution.py:31
  62.4 6.0 %collective-permute-done.40 = bf16[4,48,640]{2,1,0:T(8,128)(2,1)S(1)} collective-permute-done((bf16[4,48,640]{2,1,0:T(8,128)(2,1)S(1)}, bf16[4,48,640]{2,1,0:T(8,128)(2,1)S(1)}, u32[]{:S(2)}, u32[]{:S(2)}) %collective-permute-start.40) | collective-permute-done | bytes 245792 | tf_op jit(solution)/shard_map/ppermute | solution.py:31
  71.5 4.4 collective-permute-done.42
  94.6 5.6 %collective-permute-done.64 = bf16[4,4,32,640]{3,2,1,0:T(8,128)(2,1)S(1)} collective-permute-done((bf16[4,4,32,640]{3,2,1,0:T(8,128)(2,1)S(1)}, bf16[4,4,32,640]{3,2,1,0:T(8,128)(2,1)S(1)}, u32[]{:S(2)}, u32[]{:S(2)}) %collective-permute-start.64) | collective-permute-done | bytes 655392 | tf_op jit(solution)/shard_map/ppermute | solution.py:31
  100.3 10.4 %collective-permute-start.43 = (bf16[4,4,48,640]{3,2,1,0:T(8,128)(2,1)S(1)}, bf16[4,4,48,640]{3,2,1,0:T(8,128)(2,1)S(1)}, u32[]{:S(2)}, u32[]{:S(2)}) collective-permute-start(bf16[4,4,48,640]{3,2,1,0:T(8,128)(2,1)S(1)} %pad_maximum_fusion.2), channel_id=1, source_target_pairs={{0,16},{1,17},{2,18},{3,19},{4,20},{5,21},{6,22},{7,23},{8,24},{9,... | collective-permute-start | bytes 2949128 | tf_op jit(solution)/shard_map/ppermute | solution.py:31
  112.6 5.2 collective-permute-done.65
  121.8 8.1 %collective-permute-done.66 = bf16[2,4,32,640]{3,2,1,0:T(8,128)(2,1)S(1)} collective-permute-done((bf16[2,4,32,640]{3,2,1,0:T(8,128)(2,1)S(1)}, bf16[2,4,32,640]{3,2,1,0:T(8,128)(2,1)S(1)}, u32[]{:S(2)}, u32[]{:S(2)}) %collective-permute-start.66) | collective-permute-done | bytes 327712 | tf_op jit(solution)/shard_map/ppermute | solution.py:31
  130.1 4.0 collective-permute-start.46
  137.9 5.1 collective-permute-done.45
  155.1 5.7 %shard_map.147 = bf16[128,640]{1,0:T(8,128)(2,1)} custom-call(bf16[128,640]{1,0:T(8,128)(2,1)} %q.1, bf16[640,1280]{1,0:T(8,128)(2,1)} %copy-done.2, bf16[640,1280]{1,0:T(8,128)(2,1)} %copy-done.3, bf16[128,640]{1,0:T(8,128)(2,1)} %resid.1, s32[128,1]{1,0:T(8,128)} %copy.37.qdoc, s32[1,1280]{1,0:T(1,128)} %compare_select_fusion.kdoc, ...), custom_call_target="tpu_custom_call" | custom-call | flops 419430400 | bytes 3276800 | tf_op jit(solution)/shard_map/pallas_call | solution.py:186
  193.9 12.3 %collective-permute-done.19 = bf16[4,48,640]{2,1,0:T(8,128)(2,1)S(1)} collective-permute-done((bf16[4,48,640]{2,1,0:T(8,128)(2,1)S(1)}, bf16[4,48,640]{2,1,0:T(8,128)(2,1)S(1)}, u32[]{:S(2)}, u32[]{:S(2)}) %collective-permute-start.19) | collective-permute-done | bytes 245792 | tf_op jit(solution)/shard_map/ppermute | solution.py:31
  211.6 13.5 %collective-permute-start.34 = (bf16[2,4,32,640]{3,2,1,0:T(8,128)(2,1)S(1)}, bf16[2,4,32,640]{3,2,1,0:T(8,128)(2,1)S(1)}, u32[]{:S(2)}, u32[]{:S(2)}) collective-permute-start(bf16[2,4,32,640]{3,2,1,0:T(8,128)(2,1)S(1)} %slice.290), channel_id=1, source_target_pairs={{0,3},{1,2},{2,1},{3,0},{4,7},{5,6},{6,5},{7,4},{8,11},{9,10},{10,... | collective-permute-start | bytes 983048 | tf_op jit(solution)/shard_map/ppermute | solution.py:31
  225.3 7.5 %collective-permute-done.34 = bf16[2,4,32,640]{3,2,1,0:T(8,128)(2,1)S(1)} collective-permute-done((bf16[2,4,32,640]{3,2,1,0:T(8,128)(2,1)S(1)}, bf16[2,4,32,640]{3,2,1,0:T(8,128)(2,1)S(1)}, u32[]{:S(2)}, u32[]{:S(2)}) %collective-permute-start.34) | collective-permute-done | bytes 327712 | tf_op jit(solution)/shard_map/ppermute | solution.py:31
  234.3 22.8 %collective-permute-done.21 = bf16[4,4,48,640]{3,2,1,0:T(8,128)(2,1)S(1)} collective-permute-done((bf16[4,4,48,640]{3,2,1,0:T(8,128)(2,1)S(1)}, bf16[4,4,48,640]{3,2,1,0:T(8,128)(2,1)S(1)}, u32[]{:S(2)}, u32[]{:S(2)}) %collective-permute-start.21) | collective-permute-done | bytes 983072 | tf_op jit(solution)/shard_map/ppermute | solution.py:31
  259.8 10.1 %collective-permute-done.23 = bf16[2,4,48,640]{3,2,1,0:T(8,128)(2,1)S(1)} collective-permute-done((bf16[2,4,48,640]{3,2,1,0:T(8,128)(2,1)S(1)}, bf16[2,4,48,640]{3,2,1,0:T(8,128)(2,1)S(1)}, u32[]{:S(2)}, u32[]{:S(2)}) %collective-permute-start.23) | collective-permute-done | bytes 491552 | tf_op jit(solution)/shard_map/ppermute | solution.py:31
  273.0 8.9 %collective-permute-done.13 = bf16[2,4,48,640]{3,2,1,0:T(8,128)(2,1)S(1)} collective-permute-done((bf16[2,4,48,640]{3,2,1,0:T(8,128)(2,1)S(1)}, bf16[2,4,48,640]{3,2,1,0:T(8,128)(2,1)S(1)}, u32[]{:S(2)}, u32[]{:S(2)}) %collective-permute-start.13) | collective-permute-done | bytes 491552 | tf_op jit(solution)/shard_map/ppermute | solution.py:31
  287.1 19.3 %shard_map.148.gact = f32[1024,768]{1,0:T(8,128)} custom-call(s32[1]{0:T(128)} %bitcast.s.refs_0_, bf16[4,2,2,4,48,640]{5,4,3,2,1,0:T(8,128)(2,1)} %bitcast.339, bf16[2,2,4,4,48,640]{5,4,3,2,1,0:T(8,128)(2,1)} %bitcast.342, bf16[4,4,2,2,32,640]{5,4,3,2,1,0:T(8,128)(2,1)} %bitcast.348, bf16[2,192,5120]{2,1,0:T(8,128)(2,1)} %w0.1, bf16[2,192,5120]{2,1,0:T(8,128)(2,1)} %copy-done.14), custom_call_target="tpu_custom_call" | custom-call | flops 8053063680 | bytes 20971520 | tf_op jit(solution)/shard_map/pallas_call | solution.py:133
  306.5 38.2 %shard_map.149 = (bf16[1024,768]{1,0:T(8,128)(2,1)}, bf16[1024,768]{1,0:T(8,128)(2,1)}, bf16[768,1024]{1,0:T(8,128)(2,1)}, bf16[768,1024]{1,0:T(8,128)(2,1)}, bf16[768,1024]{1,0:T(8,128)(2,1)}) custom-call(s32[1]{0:T(128)} %bitcast.s.refs_0_, bf16[4,2,2,4,48,640]{5,4,3,2,1,0:T(8,128)(2,1)} %bitcast.333, bf16[2,2,4,4,48,640]{5,4,3,2,1,0:T(8,128)(2,1)} %bitcast.336, ...), custom_call_target="tpu_custom_call" | custom-call | flops 16106127360 | bytes 20971520 | tf_op jit(solution)/shard_map/pallas_call | solution.py:133
  344.7 29.7 %shard_map.150 = (bf16[4,2,2,4,48,640]{5,4,3,2,1,0:T(8,128)(2,1)}, bf16[2,2,4,4,48,640]{5,4,3,2,1,0:T(8,128)(2,1)}, bf16[4,4,2,2,32,640]{5,4,3,2,1,0:T(8,128)(2,1)}) custom-call(s32[1]{0:T(128)} %bitcast.s.refs_0_, bf16[1024,768]{1,0:T(8,128)(2,1)} %get-tuple-element.18.gg, bf16[1024,768]{1,0:T(8,128)(2,1)} %get-tuple-element.19.gu, ...), custom_call_target="tpu_custom_call" | custom-call | flops 16106127360 | bytes 20971520 | tf_op jit(solution)/shard_map/pallas_call | solution.py:133
  401.3 22.5 %shard_map.151 = (bf16[2,192,5120]{2,1,0:T(8,128)(2,1)}, bf16[2,192,5120]{2,1,0:T(8,128)(2,1)}, bf16[2,192,5120]{2,1,0:T(8,128)(2,1)}) custom-call(s32[1]{0:T(128)} %bitcast.s.refs_0_, f32[1,5120]{1,0:T(1,128)} %bitcast.355, bf16[4,2,2,4,48,640]{5,4,3,2,1,0:T(8,128)(2,1)} %bitcast.334, bf16[2,2,4,4,48,640]{5,4,3,2,1,0:T(8,128)(2,1)} %bitcast.337, ...), custom_call_target="tpu_custom_call" | custom-call | flops 12079595520 | bytes 20971520 | tf_op jit(solution)/shard_map/pallas_call | solution.py:133
  447.7 8.5 %collective-permute-done.78 = bf16[4,48,640]{2,1,0:T(8,128)(2,1)S(1)} collective-permute-done((bf16[4,48,640]{2,1,0:T(8,128)(2,1)S(1)}, bf16[4,48,640]{2,1,0:T(8,128)(2,1)S(1)}, u32[]{:S(2)}, u32[]{:S(2)}) %collective-permute-start.78) | collective-permute-done | bytes 245792 | tf_op jit(solution)/shard_map/ppermute | solution.py:31
  457.8 5.3 %collective-permute-done.86 = bf16[4,48,640]{2,1,0:T(8,128)(2,1)S(1)} collective-permute-done((bf16[4,48,640]{2,1,0:T(8,128)(2,1)S(1)}, bf16[4,48,640]{2,1,0:T(8,128)(2,1)S(1)}, u32[]{:S(2)}, u32[]{:S(2)}) %collective-permute-start.86) | collective-permute-done | bytes 245792 | tf_op jit(solution)/shard_map/ppermute | solution.py:31
  494.4 23.2 %shard_map.152 = (bf16[2,192,5120]{2,1,0:T(8,128)(2,1)}, bf16[2,192,5120]{2,1,0:T(8,128)(2,1)}, bf16[2,192,5120]{2,1,0:T(8,128)(2,1)}) custom-call(s32[1]{0:T(128)} %bitcast.s.refs_0_, f32[1,5120]{1,0:T(1,128)} %bitcast.356, bf16[4,2,2,4,48,640]{5,4,3,2,1,0:T(8,128)(2,1)} %bitcast.335, bf16[2,2,4,4,48,640]{5,4,3,2,1,0:T(8,128)(2,1)} %bitcast.338, ...), custom_call_target="tpu_custom_call" | custom-call | flops 12079595520 | bytes 20971520 | tf_op jit(solution)/shard_map/pallas_call | solution.py:133
  (367 shorter events, 222.3 us)
Async XLA Ops:
  31.5 61.4 %collective-permute-start.2 = (bf16[128,1280]{1,0:T(8,128)(2,1)S(1)}, bf16[128,1280]{1,0:T(8,128)(2,1)S(1)}, u32[]{:S(2)}, u32[]{:S(2)}) collective-permute-start(bf16[128,1280]{1,0:T(8,128)(2,1)S(1)} %constant_dynamic-update-slice_fusion), channel_id=1, source_target_pairs={{0,32},{8,40},{16,48},{24,56},{32,64},{40,72},{48,80},{56,88},{64,... | collective-permute-start | bytes 983048 | tf_op jit(solution)/shard_map/ppermute | solution.py:170
  36.4 54.1 %collective-permute-start.1 = (bf16[128,1280]{1,0:T(8,128)(2,1)S(1)}, bf16[128,1280]{1,0:T(8,128)(2,1)S(1)}, u32[]{:S(2)}, u32[]{:S(2)}) collective-permute-start(bf16[128,1280]{1,0:T(8,128)(2,1)S(1)} %constant_dynamic-update-slice_fusion), channel_id=1, source_target_pairs={{0,48},{8,56},{16,64},{24,72},{32,80},{40,88},{48,96},{56,104},{64... | collective-permute-start | bytes 983048 | tf_op jit(solution)/shard_map/ppermute | solution.py:170
  40.4 49.7 %collective-permute-start = (bf16[128,1280]{1,0:T(8,128)(2,1)S(1)}, bf16[128,1280]{1,0:T(8,128)(2,1)S(1)}, u32[]{:S(2)}, u32[]{:S(2)}) collective-permute-start(bf16[128,1280]{1,0:T(8,128)(2,1)S(1)} %constant_dynamic-update-slice_fusion), channel_id=1, source_target_pairs={{0,64},{8,72},{16,80},{24,88},{32,96},{40,104},{48,112},{56,120},{... | collective-permute-start | bytes 983048 | tf_op jit(solution)/shard_map/ppermute | solution.py:170
  90.1 27.7 %collective-permute-start.44 = (bf16[4,4,48,640]{3,2,1,0:T(8,128)(2,1)S(1)}, bf16[4,4,48,640]{3,2,1,0:T(8,128)(2,1)S(1)}, u32[]{:S(2)}, u32[]{:S(2)}) collective-permute-start(bf16[4,4,48,640]{3,2,1,0:T(8,128)(2,1)S(1)} %pad_maximum_fusion.2), channel_id=1, source_target_pairs={{0,48},{1,49},{2,50},{3,51},{4,52},{5,53},{6,54},{7,55},{8,56},{9,... | collective-permute-start | bytes 2949128 | tf_op jit(solution)/shard_map/ppermute | solution.py:31
  92.9 41.3 %collective-permute-start.54 = (bf16[4,4,48,640]{3,2,1,0:T(8,128)(2,1)S(1)}, bf16[4,4,48,640]{3,2,1,0:T(8,128)(2,1)S(1)}, u32[]{:S(2)}, u32[]{:S(2)}) collective-permute-start(bf16[4,4,48,640]{3,2,1,0:T(8,128)(2,1)S(1)} %pad_maximum_fusion.3), channel_id=1, source_target_pairs={{0,68},{1,69},{2,70},{3,71},{4,64},{5,65},{6,66},{7,67},{8,76},{9,... | collective-permute-start | bytes 2949128 | tf_op jit(solution)/shard_map/ppermute | solution.py:31
  100.2 36.1 %collective-permute-start.53 = (bf16[4,4,48,640]{3,2,1,0:T(8,128)(2,1)S(1)}, bf16[4,4,48,640]{3,2,1,0:T(8,128)(2,1)S(1)}, u32[]{:S(2)}, u32[]{:S(2)}) collective-permute-start(bf16[4,4,48,640]{3,2,1,0:T(8,128)(2,1)S(1)} %pad_maximum_fusion.3), channel_id=1, source_target_pairs={{0,64},{1,65},{2,66},{3,67},{4,68},{5,69},{6,70},{7,71},{8,72},{9,... | collective-permute-start | bytes 2949128 | tf_op jit(solution)/shard_map/ppermute | solution.py:31
  100.3 29.7 %collective-permute-start.43 = (bf16[4,4,48,640]{3,2,1,0:T(8,128)(2,1)S(1)}, bf16[4,4,48,640]{3,2,1,0:T(8,128)(2,1)S(1)}, u32[]{:S(2)}, u32[]{:S(2)}) collective-permute-start(bf16[4,4,48,640]{3,2,1,0:T(8,128)(2,1)S(1)} %pad_maximum_fusion.2), channel_id=1, source_target_pairs={{0,16},{1,17},{2,18},{3,19},{4,20},{5,21},{6,22},{7,23},{8,24},{9,... | collective-permute-start | bytes 2949128 | tf_op jit(solution)/shard_map/ppermute | solution.py:31
  117.8 36.2 %collective-permute-start.4 = (bf16[640,1280]{1,0:T(8,128)(2,1)S(1)}, bf16[640,1280]{1,0:T(8,128)(2,1)S(1)}, u32[]{:S(2)}, u32[]{:S(2)}) collective-permute-start(bf16[640,1280]{1,0:T(8,128)(2,1)S(1)} %constant_dynamic-update-slice_fusion.60.own), channel_id=1, source_target_pairs={{0,8},{1,9},{2,10},{3,11},{4,12},{5,13},{6,14},{7,15},{8,0},{9,1},... | collective-permute-start | bytes 4915208 | tf_op jit(solution)/shard_map/ppermute | solution.py:31
  186.1 25.0 %collective-permute-start.32 = (bf16[4,4,32,640]{3,2,1,0:T(8,128)(2,1)S(1)}, bf16[4,4,32,640]{3,2,1,0:T(8,128)(2,1)S(1)}, u32[]{:S(2)}, u32[]{:S(2)}) collective-permute-start(bf16[4,4,32,640]{3,2,1,0:T(8,128)(2,1)S(1)} %pad_maximum_fusion.8), channel_id=1, source_target_pairs={{0,3},{1,2},{2,1},{3,0},{4,7},{5,6},{6,5},{7,4},{8,11},{9,10},{10,... | collective-permute-start | bytes 1966088 | tf_op jit(solution)/shard_map/ppermute | solution.py:31
  187.3 24.2 %collective-permute-start.31 = (bf16[4,4,32,640]{3,2,1,0:T(8,128)(2,1)S(1)}, bf16[4,4,32,640]{3,2,1,0:T(8,128)(2,1)S(1)}, u32[]{:S(2)}, u32[]{:S(2)}) collective-permute-start(bf16[4,4,32,640]{3,2,1,0:T(8,128)(2,1)S(1)} %pad_maximum_fusion.8), channel_id=1, source_target_pairs={{0,1},{1,0},{2,3},{3,2},{4,5},{5,4},{6,7},{7,6},{8,9},{9,8},{10,11... | collective-permute-start | bytes 1966088 | tf_op jit(solution)/shard_map/ppermute | solution.py:31
  206.3 78.8 %collective-permute-start.67 = (bf16[2,192,5120]{2,1,0:T(8,128)(2,1)S(1)}, bf16[2,192,5120]{2,1,0:T(8,128)(2,1)S(1)}, u32[]{:S(2)}, u32[]{:S(2)}) collective-permute-start(bf16[2,192,5120]{2,1,0:T(8,128)(2,1)S(1)} %copy-done.13), channel_id=1, source_target_pairs={{0,8},{1,9},{2,10},{3,11},{4,12},{5,13},{6,14},{7,15},{8,0},{9,1},... | collective-permute-start | bytes 11796488 | tf_op jit(solution)/shard_map/ppermute | solution.py:31
  207.3 25.5 %collective-permute-start.12 = (bf16[4,4,48,640]{3,2,1,0:T(8,128)(2,1)S(1)}, bf16[4,4,48,640]{3,2,1,0:T(8,128)(2,1)S(1)}, u32[]{:S(2)}, u32[]{:S(2)}) collective-permute-start(bf16[4,4,48,640]{3,2,1,0:T(8,128)(2,1)S(1)} %pad_maximum_fusion), channel_id=1, source_target_pairs={{0,48},{1,49},{2,50},{3,51},{4,52},{5,53},{6,54},{7,55},{8,56},{9,... | collective-permute-start | bytes 2949128 | tf_op jit(solution)/shard_map/ppermute | solution.py:31
  209.7 24.3 %collective-permute-start.22 = (bf16[4,4,48,640]{3,2,1,0:T(8,128)(2,1)S(1)}, bf16[4,4,48,640]{3,2,1,0:T(8,128)(2,1)S(1)}, u32[]{:S(2)}, u32[]{:S(2)}) collective-permute-start(bf16[4,4,48,640]{3,2,1,0:T(8,128)(2,1)S(1)} %pad_maximum_fusion.1), channel_id=1, source_target_pairs={{0,68},{1,69},{2,70},{3,71},{4,64},{5,65},{6,66},{7,67},{8,76},{9,... | collective-permute-start | bytes 2949128 | tf_op jit(solution)/shard_map/ppermute | solution.py:31
  225.2 81.3 %collective-permute-start.35 = (bf16[2,192,5120]{2,1,0:T(8,128)(2,1)}, bf16[2,192,5120]{2,1,0:T(8,128)(2,1)}, u32[]{:S(2)}, u32[]{:S(2)}) collective-permute-start(bf16[2,192,5120]{2,1,0:T(8,128)(2,1)} %wg0.3), channel_id=1, source_target_pairs={{0,8},{1,9},{2,10},{3,11},{4,12},{5,13},{6,14},{7,15},{8,0},{9,1},... | collective-permute-start | bytes 11796488 | tf_op jit(solution)/shard_map/ppermute | solution.py:31
  232.7 73.7 %collective-permute-start.36 = (bf16[2,192,5120]{2,1,0:T(8,128)(2,1)}, bf16[2,192,5120]{2,1,0:T(8,128)(2,1)}, u32[]{:S(2)}, u32[]{:S(2)}) collective-permute-start(bf16[2,192,5120]{2,1,0:T(8,128)(2,1)} %wu0.3), channel_id=1, source_target_pairs={{0,8},{1,9},{2,10},{3,11},{4,12},{5,13},{6,14},{7,15},{8,0},{9,1},... | collective-permute-start | bytes 11796488 | tf_op jit(solution)/shard_map/ppermute | solution.py:31
  232.8 24.2 %collective-permute-start.21 = (bf16[4,4,48,640]{3,2,1,0:T(8,128)(2,1)S(1)}, bf16[4,4,48,640]{3,2,1,0:T(8,128)(2,1)S(1)}, u32[]{:S(2)}, u32[]{:S(2)}) collective-permute-start(bf16[4,4,48,640]{3,2,1,0:T(8,128)(2,1)S(1)} %pad_maximum_fusion.1), channel_id=1, source_target_pairs={{0,64},{1,65},{2,66},{3,67},{4,68},{5,69},{6,70},{7,71},{8,72},{9,... | collective-permute-start | bytes 2949128 | tf_op jit(solution)/shard_map/ppermute | solution.py:31
  234.1 23.4 %collective-permute-start.11 = (bf16[4,4,48,640]{3,2,1,0:T(8,128)(2,1)S(1)}, bf16[4,4,48,640]{3,2,1,0:T(8,128)(2,1)S(1)}, u32[]{:S(2)}, u32[]{:S(2)}) collective-permute-start(bf16[4,4,48,640]{3,2,1,0:T(8,128)(2,1)S(1)} %pad_maximum_fusion), channel_id=1, source_target_pairs={{0,16},{1,17},{2,18},{3,19},{4,20},{5,21},{6,22},{7,23},{8,24},{9,... | collective-permute-start | bytes 2949128 | tf_op jit(solution)/shard_map/ppermute | solution.py:31
  390.1 33.7 %collective-permute-start.93 = (bf16[4,4,32,640]{3,2,1,0:T(8,128)(2,1)}, bf16[4,4,32,640]{3,2,1,0:T(8,128)(2,1)}, u32[]{:S(2)}, u32[]{:S(2)}) collective-permute-start(bf16[4,4,32,640]{3,2,1,0:T(8,128)(2,1)} %pad_maximum_fusion.10), channel_id=1, source_target_pairs={{0,1},{1,0},{2,3},{3,2},{4,5},{5,4},{6,7},{7,6},{8,9},{9,8},{10,11... | collective-permute-start | bytes 1966088 | tf_op jit(solution)/shard_map/ppermute | solution.py:31
  392.7 36.5 %collective-permute-start.75 = (bf16[4,4,48,640]{3,2,1,0:T(8,128)(2,1)}, bf16[4,4,48,640]{3,2,1,0:T(8,128)(2,1)}, u32[]{:S(2)}, u32[]{:S(2)}) collective-permute-start(bf16[4,4,48,640]{3,2,1,0:T(8,128)(2,1)} %pad_maximum_fusion.5), channel_id=1, source_target_pairs={{0,48},{1,49},{2,50},{3,51},{4,52},{5,53},{6,54},{7,55},{8,56},{9,... | collective-permute-start | bytes 2949128 | tf_op jit(solution)/shard_map/ppermute | solution.py:31
  394.9 34.4 %collective-permute-start.73 = (bf16[4,4,48,640]{3,2,1,0:T(8,128)(2,1)}, bf16[4,4,48,640]{3,2,1,0:T(8,128)(2,1)}, u32[]{:S(2)}, u32[]{:S(2)}) collective-permute-start(bf16[4,4,48,640]{3,2,1,0:T(8,128)(2,1)} %pad_maximum_fusion.4), channel_id=1, source_target_pairs={{0,16},{1,17},{2,18},{3,19},{4,20},{5,21},{6,22},{7,23},{8,24},{9,... | collective-permute-start | bytes 2949128 | tf_op jit(solution)/shard_map/ppermute | solution.py:31
  396.3 27.6 %collective-permute-start.85 = (bf16[4,4,48,640]{3,2,1,0:T(8,128)(2,1)}, bf16[4,4,48,640]{3,2,1,0:T(8,128)(2,1)}, u32[]{:S(2)}, u32[]{:S(2)}) collective-permute-start(bf16[4,4,48,640]{3,2,1,0:T(8,128)(2,1)} %pad_maximum_fusion.7), channel_id=1, source_target_pairs={{0,68},{1,69},{2,70},{3,71},{4,64},{5,65},{6,66},{7,67},{8,76},{9,... | collective-permute-start | bytes 2949128 | tf_op jit(solution)/shard_map/ppermute | solution.py:31
  423.8 70.6 %collective-permute-start.102 = (bf16[2,192,5120]{2,1,0:T(8,128)(2,1)}, bf16[2,192,5120]{2,1,0:T(8,128)(2,1)}, u32[]{:S(2)}, u32[]{:S(2)}) collective-permute-start(bf16[2,192,5120]{2,1,0:T(8,128)(2,1)} %get-tuple-element.26), channel_id=1, source_target_pairs={{0,8},{1,9},{2,10},{3,11},{4,12},{5,13},{6,14},{7,15},{8,0},{9,1},... | collective-permute-start | bytes 11796488 | tf_op jit(solution)/shard_map/ppermute | solution.py:31
  423.9 70.5 %collective-permute-start.103 = (bf16[2,192,5120]{2,1,0:T(8,128)(2,1)}, bf16[2,192,5120]{2,1,0:T(8,128)(2,1)}, u32[]{:S(2)}, u32[]{:S(2)}) collective-permute-start(bf16[2,192,5120]{2,1,0:T(8,128)(2,1)} %get-tuple-element.27), channel_id=1, source_target_pairs={{0,8},{1,9},{2,10},{3,11},{4,12},{5,13},{6,14},{7,15},{8,0},{9,1},... | collective-permute-start | bytes 11796488 | tf_op jit(solution)/shard_map/ppermute | solution.py:31
  424.4 70.0 %collective-permute-start.104 = (bf16[2,192,5120]{2,1,0:T(8,128)(2,1)}, bf16[2,192,5120]{2,1,0:T(8,128)(2,1)}, u32[]{:S(2)}, u32[]{:S(2)}) collective-permute-start(bf16[2,192,5120]{2,1,0:T(8,128)(2,1)} %get-tuple-element.28), channel_id=1, source_target_pairs={{0,8},{1,9},{2,10},{3,11},{4,12},{5,13},{6,14},{7,15},{8,0},{9,1},... | collective-permute-start | bytes 11796488 | tf_op jit(solution)/shard_map/ppermute | solution.py:31
  (96 other events, 1139.3 us)

commit v3 on v2

--- a/solution.py
+++ b/solution.py
@@ -46,9 +46,10 @@
     return sum(t.astype(F32) for t in terms).astype(BF16)
 
 
-def scatter_ring(p, mask):
+def scatter_ring(p, mask, tie):
     half = p.shape[1] // 2
     from_one, from_three = swap(p[2, :half], mask(1)), swap(p[2, half:], mask(3))
+    from_one, from_three = tie(from_one, from_three)
     for_one = jnp.concatenate([p[1, :half], add(p[1, half:], from_three)])
     for_three = jnp.concatenate([add(p[3, :half], from_one), p[3, half:]])
     return add(p[0], swap(for_one, mask(1)), swap(for_three, mask(3)))
@@ -81,23 +82,35 @@
     )
 
 
-def scatter_tokens(parts):
-    outs = []
-    for part, (first, second, last) in zip(parts, ORDERS):
-        part = part.reshape(4, 4, 4, *part.shape[-2:])
-        part = scatter_ring(part, last)
-        part = scatter_direct(part, second)
-        outs.append(scatter_direct(part, first))
-    return jnp.concatenate(outs)
-
-
-def part_specs(sizes, width):
+def scatter_part(part, order, tie):
+    first, second, last = order
+    part = part.reshape(4, 4, 4, *part.shape[-2:])
+    return scatter_direct(scatter_direct(scatter_ring(part, last, tie), second), first)
+
+
+def part_specs(sizes, width, side=0):
     a, b, c = sizes
     return [
-        pl.BlockSpec((4, None, 2, None, a, width), lambda f, s: (0, f // 4, 0, f % 4, 0, 0)),
-        pl.BlockSpec((None, 2, None, 4, b, width), lambda f, s: (f // 4, 0, f % 4, 0, 0, 0)),
-        pl.BlockSpec((None, 4, None, 2, c, width), lambda f, s: (f % 4, 0, f // 4, 0, 0, 0)),
+        pl.BlockSpec((4, None, 2, 2, a, width), lambda f, s: (0, f // 2, 0, f % 2, 0, side)),
+        pl.BlockSpec((None, 2, 2, 4, b, width), lambda f, s: (f // 2, 0, f % 2, 0, 0, side)),
+        pl.BlockSpec((2, 4, None, 2, c, width), lambda f, s: (f % 2, 0, f // 2, 0, 0, side)),
     ]
+
+
+PAIR_AXES = (2, 1, 0)
+
+
+def pair_at(axis, i):
+    return (slice(None),) * axis + (i,)
+
+
+def pair_rows(ref, axis, odd):
+    sides = [ref[pair_at(axis, i)].reshape(-1, ref.shape[-1]) for i in (odd, 1 - odd)]
+    return jnp.concatenate(sides, axis=1)
+
+
+def stacked(*refs):
+    return jnp.concatenate([rows_of(r) for r in refs])
 
 
 def part_shapes(sizes, width):
@@ -122,7 +135,7 @@
 
 
 def weight_spec(w, width):
-    return pl.BlockSpec((w.shape[0], w.shape[1], width), lambda f, s: (0, 0, f ^ s[0]))
+    return pl.BlockSpec((w.shape[0], w.shape[1], 2 * width), lambda f, s: (0, 0, f ^ (s[0] // 2)))
 
 
 def whole(shape):
@@ -145,8 +158,9 @@
     )(col, *args)
 
 
-def attention_kernel(q, own, sib, resid, qdoc, kdoc, qpos, kpos, out):
+def attention_kernel(q, own, sib, resid, cot, qdoc, kdoc, qpos, kpos, out):
     width = q.shape[1]
+    out[:, :width] = cot[...]
     keys = own.shape[0]
     delta = qpos[...] - kpos[...]
     allowed = (delta >= 0) & (delta < WINDOW) & (qdoc[...] == kdoc[...])
@@ -158,10 +172,10 @@
         e = jnp.exp(s - jnp.max(s, axis=1, keepdims=True))
         p = (e / jnp.sum(e, axis=1, keepdims=True)).astype(BF16)
         o = dot_nn(p[:, :keys], own[:, vcols]) + dot_nn(p[:, keys:], sib[:, vcols])
-        out[:, cols] = (resid[:, cols].astype(F32) + o).astype(BF16)
-
-
-def attend(queries, keys, values, resid, doc_ids, row):
+        out[:, vcols] = (resid[:, cols].astype(F32) + o).astype(BF16)
+
+
+def attend(queries, keys, values, resid, cotangent, doc_ids, row):
     rows, width = queries.shape
     reach = WINDOW // rows
     pair = jnp.concatenate([keys, values], axis=1)
@@ -185,59 +199,50 @@
     qpos = row * rows + jnp.arange(rows, dtype=jnp.int32)[:, None]
     return pl.pallas_call(
         attention_kernel,
-        out_shape=jax.ShapeDtypeStruct((rows, width), BF16),
+        out_shape=jax.ShapeDtypeStruct((rows, 2 * width), BF16),
         compiler_params=pltpu.CompilerParams(vmem_limit_bytes=VMEM),
         cost_estimate=pl.CostEstimate(flops=4 * rows * width * own.shape[0] * 2, bytes_accessed=4 * own.size, transcendentals=0),
-    )(queries, own, sib, resid, qdoc, kdoc, qpos, kpos)
-
-
-def grad_act_kernel(s, xa, xb, xc, w0, w1, out):
-    @pl.when(pl.program_id(0) == 0)
-    def _():
-        out[...] = jnp.zeros_like(out)
-
-    n = out.shape[1] // 2
-    start = 0
-    for x in (xa, xb, xc):
-        x = rows_of(x)
-        span = slice(start, start + x.shape[0])
-        start += x.shape[0]
-        out[span, :n] += dot_nt(x, rows_of(w0))
-        out[span, n:] += dot_nt(x, rows_of(w1))
+    )(queries, own, sib, resid, cotangent, qdoc, kdoc, qpos, kpos)
 
 
 def hidden_kernel(
-    s, xa, xb, xc, wg0, wg1, wu0, wu1, gain, gact, gates, gg_out, gu_out, act_t, gg_t, gu_t, g_acc, u_acc, sq_acc
+    s, ca, cb, cc, xa, xb, xc, wg0, wg1, wu0, wu1, wd0, wd1, gain, gates,
+    gg_out, gu_out, act_t, gg_t, gu_t, g_acc, u_acc, d_acc, sq_acc
 ):
     f = pl.program_id(0)
     tokens, hidden = g_acc.shape
-    n = hidden // 2
+    odd = s[0] % 2
+
+    def products(first):
+        start = 0
+        for axis, c, x in zip(PAIR_AXES, (ca, cb, cc), (xa, xb, xc)):
+            x = pair_rows(x, axis, odd).astype(F32)
+            span = slice(start, start + x.shape[0])
+            start += x.shape[0]
+            sq = x * x
+            total = sq[:, :128]
+            for j in range(128, x.shape[1], 128):
+                total += sq[:, j : j + 128]
+            x = (x * gain[...]).astype(BF16)
+            for acc, value in (
+                (sq_acc, total),
+                (g_acc, dot_nt(x, stacked(wg0, wg1))),
+                (u_acc, dot_nt(x, stacked(wu0, wu1))),
+                (d_acc, dot_nt(pair_rows(c, axis, odd), stacked(wd0, wd1))),
+            ):
+                acc[span] = value if first else acc[span] + value
 
     @pl.when(f == 0)
     def _():
-        g_acc[...] = jnp.zeros_like(g_acc)
-        u_acc[...] = jnp.zeros_like(u_acc)
-        sq_acc[...] = jnp.zeros_like(sq_acc)
-
-    start = 0
-    for x in (xa, xb, xc):
-        x = rows_of(x).astype(F32)
-        span = slice(start, start + x.shape[0])
-        start += x.shape[0]
-        sq = x * x
-        total = sq[:, :128]
-        for j in range(128, x.shape[1], 128):
-            total += sq[:, j : j + 128]
-        sq_acc[span] += total
-        x = (x * gain[...]).astype(BF16)
-        g_acc[span, :n] += dot_nt(x, rows_of(wg0))
-        g_acc[span, n:] += dot_nt(x, rows_of(wg1))
-        u_acc[span, :n] += dot_nt(x, rows_of(wu0))
-        u_acc[span, n:] += dot_nt(x, rows_of(wu1))
+        products(True)
+
+    @pl.when(f > 0)
+    def _():
+        products(False)
 
     @pl.when(f == pl.num_programs(0) - 1)
     def _():
-        feats = pl.num_programs(0) * xa.shape[-1]
+        feats = pl.num_programs(0) * 2 * xa.shape[-1]
         expert = lax.broadcasted_iota(jnp.int32, (1, hidden), 1) // (hidden // 4)
         for r in range(0, tokens, 128):
             span = slice(r, r + 128)
@@ -250,7 +255,7 @@
             pre_gate, pre_up = g_acc[span] * inv, u_acc[span] * inv
             sig = jax.nn.sigmoid(pre_gate)
             silu = pre_gate * sig
-            grad = gact[span] * gate
+            grad = d_acc[span] * gate
             gg = grad * pre_up * sig * (1.0 + pre_gate * (1.0 - sig))
             gu = grad * silu
             gg_out[span] = gg.astype(BF16)
@@ -260,16 +265,13 @@
             gu_t[:, span] = (gu * inv).T.astype(BF16)
 
 
-def piece_kernel(s, gg, gu, wg0, wg1, wu0, wu1, oa, ob, oc):
-    n = gg.shape[1] // 2
-    start = 0
-    for o in (oa, ob, oc):
-        size = o.shape[0] * o.shape[1] * o.shape[2]
-        span = slice(start, start + size)
-        start += size
-        out = dot_nn(gg[span, :n], rows_of(wg0)) + dot_nn(gg[span, n:], rows_of(wg1))
-        out += dot_nn(gu[span, :n], rows_of(wu0)) + dot_nn(gu[span, n:], rows_of(wu1))
-        o[...] = out.astype(BF16).reshape(o.shape)
+def piece_kernel(axis, s, gg, gu, wg0, wg1, wu0, wu1, o):
+    odd = s[0] % 2
+    width = o.shape[-1]
+    out = dot_nn(gg[...], stacked(wg0, wg1)) + dot_nn(gu[...], stacked(wu0, wu1))
+    for i, at in enumerate((odd, 1 - odd)):
+        at = pair_at(axis, at)
+        o[at] = out[:, i * width : (i + 1) * width].astype(BF16).reshape(o.at[at].shape)
 
 
 def weight_grad_kernel(with_more, s, gain, *refs):
@@ -277,18 +279,14 @@
     act_t, gg_t, gu_t = refs[6:9]
     more = refs[9:12] if with_more else (None,) * 3
     dg, du, dd = refs[-3:]
+    odd = s[0] % 2
     for lhs, data, scale, extra, out in (
         (gg_t, xs, gain, more[0], dg),
         (gu_t, xs, gain, more[1], du),
         (act_t, cs, None, more[2], dd),
     ):
-        start = 0
-        total = None
-        for x in data:
-            x = rows_of(x)
-            term = dot_nn(lhs[:, start : start + x.shape[0]], x)
-            start += x.shape[0]
-            total = term if total is None else total + term
+        rows = jnp.concatenate([pair_rows(x, axis, odd) for axis, x in zip(PAIR_AXES, data)])
+        total = dot_nn(lhs[...], rows)
         if scale is not None:
             total = total * scale[...]
         if extra is not None:
@@ -302,13 +300,13 @@
     rows, width = queries.shape
     row, col = lax.axis_index("row"), lax.axis_index("col")
     experts, inner, feats = w_gate.shape
-    steps = feats // width
+    steps = feats // width // 2
     hidden = 2 * experts * inner
     tokens = 8 * rows
     sizes = [size for _, size in split_rows(rows)]
     here = jnp.reshape(col, (1,)).astype(jnp.int32)
 
-    hidden_in = attend(queries, keys, values, resid, doc_ids, row)
+    paired = attend(queries, keys, values, resid, cotangent, doc_ids, row)
     ids = jnp.arange(16 * experts, dtype=jnp.int32)
     table = jnp.sum(
         jnp.where(expert_ids[:, :, None] == ids, gate_levels[:, :, None].astype(F32) / 64.0, 0.0), axis=1
@@ -325,44 +323,49 @@
     ).astype(F32)
 
     sib_down, sib_gate, sib_up = swap(w_down, CORE), swap(w_gate, CORE), swap(w_up, CORE)
-    cot = gather_tokens(cotangent)
-    x = gather_tokens(hidden_in)
+    x = gather_tokens(paired)
     gain = norm_gain.reshape(1, feats)
 
-    xs = part_specs(sizes, width)
+    cs, xs = part_specs(sizes, width, 0), part_specs(sizes, width, 1)
     ws = weight_spec(w_gate, width)
-    gain_spec = pl.BlockSpec((1, width), lambda f, s: (0, f ^ s[0]))
+    gain_spec = pl.BlockSpec((1, 2 * width), lambda f, s: (0, f ^ (s[0] // 2)))
     one = 2 * tokens * hidden * feats
-    grad_act = call(
-        grad_act_kernel, here, steps, xs + [ws] * 2, whole((tokens, hidden)),
-        jax.ShapeDtypeStruct((tokens, hidden), F32), [], (*cot, w_down, sib_down), one, 2 * tokens * feats * 2,
-    )
     flat = jax.ShapeDtypeStruct((tokens, hidden), BF16)
     turned = jax.ShapeDtypeStruct((hidden, tokens), BF16)
+    kept = pl.BlockSpec(memory_space=pltpu.VMEM)
     gg, gu, act_t, gg_t, gu_t = call(
         hidden_kernel, here, steps,
-        xs + [ws] * 4 + [gain_spec, whole((tokens, hidden)), whole((tokens, 4))],
-        [whole((tokens, hidden))] * 2 + [whole((hidden, tokens))] * 3,
-        [flat, flat, turned, turned, turned],
-        [pltpu.VMEM((tokens, hidden), F32), pltpu.VMEM((tokens, hidden), F32), pltpu.VMEM((tokens, 128), F32)],
-        (*x, w_gate, sib_gate, w_up, sib_up, gain, grad_act, gates), 2 * one, 4 * tokens * feats,
+        cs + xs + [ws] * 6 + [gain_spec, whole((tokens, 4))],
+        [kept] * 5, [flat, flat, turned, turned, turned],
+        [pltpu.VMEM((tokens, hidden), F32)] * 3 + [pltpu.VMEM((tokens, 128), F32)],
+        (*x, *x, w_gate, sib_gate, w_up, sib_up, w_down, sib_down, gain, gates), 3 * one, 8 * tokens * feats,
     )
-    pieces = call(
-        piece_kernel, here, steps, [whole((tokens, hidden))] * 2 + [ws] * 4, xs, part_shapes(sizes, width), [],
-        (gg, gu, w_gate, sib_gate, w_up, sib_up), 2 * one, 4 * tokens * feats,
-    )
-    d_normed = scatter_tokens(pieces)
+    pieces = []
+    outs = part_specs(sizes, width)
+    for i, (start, size) in enumerate(split_rows(rows)):
+        rows_spec = pl.BlockSpec((8 * size, hidden), lambda f, s, at=start // size: (at, 0))
+        pieces.append(
+            call(
+                lambda *refs, axis=PAIR_AXES[i]: piece_kernel(axis, *refs), here, steps,
+                [rows_spec] * 2 + [ws] * 4, outs[i], part_shapes(sizes, width)[i], [],
+                (gg, gu, w_gate, sib_gate, w_up, sib_up), 2 * one * size // rows, 8 * hidden * feats,
+            )
+        )
 
     def weight_grads(which, more):
         half = pl.BlockSpec((hidden // 2, tokens), lambda f, s: (which, 0))
         return call(
             lambda *refs: weight_grad_kernel(bool(more), *refs), here, steps,
-            [gain_spec] + xs * 2 + [half] * 3 + [ws] * len(more), [ws] * 3,
+            [gain_spec] + xs + cs + [half] * 3 + [ws] * len(more), [ws] * 3,
             [jax.ShapeDtypeStruct(w_gate.shape, BF16)] * 3, [],
-            (gain, *x, *cot, act_t, gg_t, gu_t, *more), 3 * one // 2, 4 * tokens * feats,
+            (gain, *x, *x, act_t, gg_t, gu_t, *more), 3 * one // 2, 8 * tokens * feats,
         )
 
     sent = weight_grads(1, ())
+    sums = []
+    for part, order in zip(pieces, ORDERS):
+        sums.append(scatter_part(part, order, lambda a, b: lax.optimization_barrier((a, b, sent[0][:1, :1, :128]))[:2]))
+    d_normed = jnp.concatenate(sums)
     d_gate, d_up, d_down = weight_grads(0, tuple(swap(d, CORE) for d in sent))
     return (d_normed, d_gate, d_up, d_down)
 

time: 527 us -> 465 us (0.88)
  starting transfers between devices: 153 us -> 109 us
  Pallas kernels: 139 us -> 114 us
  other arithmetic: 17.5 us -> 8.22 us
  waiting for transfers between devices: 181 us -> 190 us
  local copies, waits for them, and re-layouts: 25.5 us -> 33.8 us
    ppermute x101 -> x71, starting transfers between devices: 141 us -> 96.1 us  [swap(): return lax.ppermute(x, ('row', 'col'), [(i, i ^ mask) for i in range(128)])]
    pallas_call x5 -> x6, Pallas kernels: 133 us -> 108 us  [call(): pl.pallas_call(kernel, out_shape=out_shape, grid_spec=pltpu.PrefetchScala...]
    ppermute x4, waiting for transfers between devices: 0.01 us -> 15 us  [attend(): lax.ppermute(pair, 'row', [(i, i + by) for i in range(16 - by)])]
    unnamed x75 -> x69, local copies, waits for them, and re-layouts: 10 us -> 18.7 us
    ppermute x101 -> x71, waiting for transfers between devices: 181 us -> 175 us  [swap(): return lax.ppermute(x, ('row', 'col'), [(i, i ^ mask) for i in range(128)])]
  transfers between devices with their start and end apart: 105 -> 75, of which waited for: 44 -> 35; matrix products, arithmetic and copies ran while one was open for 6% -> 6% of each run, Pallas kernels for 8% -> 9%
where the time goes in v3:
time: 465 us; the launch traced here: 456 us
  waiting for transfers between devices  190 us (41%)
  Pallas kernels  114 us (25%)
  starting transfers between devices  109 us (23%)
  local copies, waits for them, and re-layouts  33.8 us (7%)
  other arithmetic  8.22 us (2%)
    ppermute x71, waiting for transfers between devices, swap(): return lax.ppermute(x, ('row', 'col'), [(i, i ^ mask) for i in range(128)])  175 us
    pallas_call x6, Pallas kernels, call(): pl.pallas_call(kernel, out_shape=out_shape, grid_spec=pltpu.PrefetchScala...  108 us
    ppermute x71, starting transfers between devices, swap(): return lax.ppermute(x, ('row', 'col'), [(i, i ^ mask) for i in range(128)])  96.1 us
    unnamed x69, local copies, waits for them, and re-layouts  18.7 us
    ppermute x4, waiting for transfers between devices, attend(): lax.ppermute(pair, 'row', [(i, i + by) for i in range(16 - by)])  15 us
    ppermute x4, starting transfers between devices, attend(): lax.ppermute(pair, 'row', [(i, i + by) for i in range(16 - by)])  13 us
  transfers between devices with their start and end apart: 75, of which 35 were waited for; matrix products, arithmetic and copies ran while one was open for 6% of the time, Pallas kernels for 9%

profile of v3, /device:TPU:0, one launch (start us, length us, event | category | flops | bytes accessed | tf_op | source)
XLA Modules:
  0.0 456.3 jit_solution(10355308898178726503)
XLA Ops:
  19.1 15.0 %collective-permute-done = bf16[128,1280]{1,0:T(8,128)(2,1)S(1)} collective-permute-done((bf16[128,1280]{1,0:T(8,128)(2,1)S(1)}, bf16[128,1280]{1,0:T(8,128)(2,1)S(1)}, u32[]{:S(2)}, u32[]{:S(2)}) %collective-permute-start) | collective-permute-done | bytes 327712 | tf_op jit(solution)/shard_map/ppermute | solution.py:184
  46.7 5.8 %shard_map.147 = bf16[128,1280]{1,0:T(8,128)(2,1)} custom-call(bf16[128,640]{1,0:T(8,128)(2,1)} %q.1, bf16[640,1280]{1,0:T(8,128)(2,1)} %copy-done.11, bf16[640,1280]{1,0:T(8,128)(2,1)} %copy-done.16, bf16[128,640]{1,0:T(8,128)(2,1)} %resid.1, bf16[128,640]{1,0:T(8,128)(2,1)} %cot.1, s32[128,1]{1,0:T(8,128)} %copy.37.qdoc, ...), custom_call_target="tpu_custom_call" | custom-call | flops 419430400 | bytes 3276800 | tf_op jit(solution)/shard_map/pallas_call | solution.py:200
  100.5 14.8 %collective-permute-start.31 = (bf16[4,4,32,1280]{3,2,1,0:T(8,128)(2,1)S(1)}, bf16[4,4,32,1280]{3,2,1,0:T(8,128)(2,1)S(1)}, u32[]{:S(2)}, u32[]{:S(2)}) collective-permute-start(bf16[4,4,32,1280]{3,2,1,0:T(8,128)(2,1)S(1)} %pad_maximum_fusion.2), channel_id=1, source_target_pairs={{0,1},{1,0},{2,3},{3,2},{4,5},{5,4},{6,7},{7,6},{8,9},{9,8},{10,11... | collective-permute-start | bytes 3932168 | tf_op jit(solution)/shard_map/ppermute | solution.py:31
  119.2 19.4 %collective-permute-done.20 = bf16[4,48,1280]{2,1,0:T(8,128)(2,1)S(1)} collective-permute-done((bf16[4,48,1280]{2,1,0:T(8,128)(2,1)S(1)}, bf16[4,48,1280]{2,1,0:T(8,128)(2,1)S(1)}, u32[]{:S(2)}, u32[]{:S(2)}) %collective-permute-start.20) | collective-permute-done | bytes 491552 | tf_op jit(solution)/shard_map/ppermute | solution.py:31
  141.5 6.3 %collective-permute-start.22 = (bf16[4,4,48,1280]{3,2,1,0:T(8,128)(2,1)S(1)}, bf16[4,4,48,1280]{3,2,1,0:T(8,128)(2,1)S(1)}, u32[]{:S(2)}, u32[]{:S(2)}) collective-permute-start(bf16[4,4,48,1280]{3,2,1,0:T(8,128)(2,1)S(1)} %pad_maximum_fusion.1), channel_id=1, source_target_pairs={{0,68},{1,69},{2,70},{3,71},{4,64},{5,65},{6,66},{7,67},{8,76},{9,... | collective-permute-start | bytes 5898248 | tf_op jit(solution)/shard_map/ppermute | solution.py:31
  147.8 5.1 %collective-permute-done.33 = bf16[2,4,32,1280]{3,2,1,0:T(8,128)(2,1)S(1)} collective-permute-done((bf16[2,4,32,1280]{3,2,1,0:T(8,128)(2,1)S(1)}, bf16[2,4,32,1280]{3,2,1,0:T(8,128)(2,1)S(1)}, u32[]{:S(2)}, u32[]{:S(2)}) %collective-permute-start.33) | collective-permute-done | bytes 655392 | tf_op jit(solution)/shard_map/ppermute | solution.py:31
  156.6 9.4 %collective-permute-done.34 = bf16[2,4,32,1280]{3,2,1,0:T(8,128)(2,1)S(1)} collective-permute-done((bf16[2,4,32,1280]{3,2,1,0:T(8,128)(2,1)S(1)}, bf16[2,4,32,1280]{3,2,1,0:T(8,128)(2,1)S(1)}, u32[]{:S(2)}, u32[]{:S(2)}) %collective-permute-start.34) | collective-permute-done | bytes 655392 | tf_op jit(solution)/shard_map/ppermute | solution.py:31
  168.3 11.8 %collective-permute-done.21 = bf16[4,4,48,1280]{3,2,1,0:T(8,128)(2,1)S(1)} collective-permute-done((bf16[4,4,48,1280]{3,2,1,0:T(8,128)(2,1)S(1)}, bf16[4,4,48,1280]{3,2,1,0:T(8,128)(2,1)S(1)}, u32[]{:S(2)}, u32[]{:S(2)}) %collective-permute-start.21) | collective-permute-done | bytes 1966112 | tf_op jit(solution)/shard_map/ppermute | solution.py:31
  181.4 6.9 %collective-permute-done.22 = bf16[4,4,48,1280]{3,2,1,0:T(8,128)(2,1)S(1)} collective-permute-done((bf16[4,4,48,1280]{3,2,1,0:T(8,128)(2,1)S(1)}, bf16[4,4,48,1280]{3,2,1,0:T(8,128)(2,1)S(1)}, u32[]{:S(2)}, u32[]{:S(2)}) %collective-permute-start.22) | collective-permute-done | bytes 1966112 | tf_op jit(solution)/shard_map/ppermute | solution.py:31
  188.6 9.9 %collective-permute-done.13 = bf16[2,4,48,1280]{3,2,1,0:T(8,128)(2,1)S(1)} collective-permute-done((bf16[2,4,48,1280]{3,2,1,0:T(8,128)(2,1)S(1)}, bf16[2,4,48,1280]{3,2,1,0:T(8,128)(2,1)S(1)}, u32[]{:S(2)}, u32[]{:S(2)}) %collective-permute-start.13) | collective-permute-done | bytes 983072 | tf_op jit(solution)/shard_map/ppermute | solution.py:31
  200.1 10.0 %collective-permute-done.14 = bf16[2,4,48,1280]{3,2,1,0:T(8,128)(2,1)S(1)} collective-permute-done((bf16[2,4,48,1280]{3,2,1,0:T(8,128)(2,1)S(1)}, bf16[2,4,48,1280]{3,2,1,0:T(8,128)(2,1)S(1)}, u32[]{:S(2)}, u32[]{:S(2)}) %collective-permute-start.14) | collective-permute-done | bytes 983072 | tf_op jit(solution)/shard_map/ppermute | solution.py:31
  217.5 13.4 %collective-permute-done.24 = bf16[2,4,48,1280]{3,2,1,0:T(8,128)(2,1)S(1)} collective-permute-done((bf16[2,4,48,1280]{3,2,1,0:T(8,128)(2,1)S(1)}, bf16[2,4,48,1280]{3,2,1,0:T(8,128)(2,1)S(1)}, u32[]{:S(2)}, u32[]{:S(2)}) %collective-permute-start.24) | collective-permute-done | bytes 983072 | tf_op jit(solution)/shard_map/ppermute | solution.py:31
  238.3 38.2 %shard_map.148 = (bf16[1024,768]{1,0:T(8,128)(2,1)}, bf16[1024,768]{1,0:T(8,128)(2,1)}, bf16[768,1024]{1,0:T(8,128)(2,1)}, bf16[768,1024]{1,0:T(8,128)(2,1)}, bf16[768,1024]{1,0:T(8,128)(2,1)}) custom-call(s32[1]{0:T(128)} %bitcast.s.refs_0_, bf16[4,2,2,4,48,1280]{5,4,3,2,1,0:T(8,128)(2,1)} %bitcast.219, ...), custom_call_target="tpu_custom_call" | custom-call | flops 24159191040 | bytes 41943040 | tf_op jit(solution)/shard_map/pallas_call | solution.py:146
  276.5 9.8 %shard_map.152 = bf16[4,4,2,2,32,640]{5,4,3,2,1,0:T(8,128)(2,1)} custom-call(s32[1]{0:T(128)} %bitcast.s.refs_0_, bf16[1024,768]{1,0:T(8,128)(2,1)} %get-tuple-element.21.refs_1_, bf16[1024,768]{1,0:T(8,128)(2,1)} %get-tuple-element.22.refs_2_, bf16[2,192,5120]{2,1,0:T(8,128)(2,1)} %refs_3_.5, bf16[2,192,5120]{2,1,0:T(8,128)(2,1)} %copy-done.4, ...), custom_call_target="tpu_custom_call" | custom-call | flops 4026531840 | bytes 31457280 | tf_op jit(solution)/shard_map/pallas_call | solution.py:146
  291.7 11.5 %shard_map.151 = bf16[2,2,4,4,48,640]{5,4,3,2,1,0:T(8,128)(2,1)} custom-call(s32[1]{0:T(128)} %bitcast.s.refs_0_, bf16[1024,768]{1,0:T(8,128)(2,1)} %get-tuple-element.21.refs_1_, bf16[1024,768]{1,0:T(8,128)(2,1)} %get-tuple-element.22.refs_2_, bf16[2,192,5120]{2,1,0:T(8,128)(2,1)} %refs_3_.5, bf16[2,192,5120]{2,1,0:T(8,128)(2,1)} %copy-done.4, ...), custom_call_target="tpu_custom_call" | custom-call | flops 6039797760 | bytes 31457280 | tf_op jit(solution)/shard_map/pallas_call | solution.py:146
  307.3 17.9 %shard_map.150 = (bf16[2,192,5120]{2,1,0:T(8,128)(2,1)}, bf16[2,192,5120]{2,1,0:T(8,128)(2,1)}, bf16[2,192,5120]{2,1,0:T(8,128)(2,1)}) custom-call(s32[1]{0:T(128)} %bitcast.s.refs_0_, f32[1,5120]{1,0:T(1,128)} %bitcast.269, bf16[4,2,2,4,48,1280]{5,4,3,2,1,0:T(8,128)(2,1)} %bitcast.221, bf16[2,2,4,4,48,1280]{5,4,3,2,1,0:T(8,128)(2,1)} %bitcast.21.cb.xb.refs_3_.refs_6_, ...), custom_call_target="tpu_custom_call" | custom-call | flops 12079595520 | bytes 41943040 | tf_op jit(solution)/shard_map/pallas_call | solution.py:146
  325.2 11.5 %shard_map.149 = bf16[4,2,2,4,48,640]{5,4,3,2,1,0:T(8,128)(2,1)} custom-call(s32[1]{0:T(128)} %bitcast.s.refs_0_, bf16[1024,768]{1,0:T(8,128)(2,1)} %get-tuple-element.21.refs_1_, bf16[1024,768]{1,0:T(8,128)(2,1)} %get-tuple-element.22.refs_2_, bf16[2,192,5120]{2,1,0:T(8,128)(2,1)} %refs_3_.5, bf16[2,192,5120]{2,1,0:T(8,128)(2,1)} %copy-done.4, ...), custom_call_target="tpu_custom_call" | custom-call | flops 6039797760 | bytes 31457280 | tf_op jit(solution)/shard_map/pallas_call | solution.py:146
  360.3 13.1 %collective-permute-done.45 = bf16[4,4,48,640]{3,2,1,0:T(8,128)(2,1)S(1)} collective-permute-done((bf16[4,4,48,640]{3,2,1,0:T(8,128)(2,1)S(1)}, bf16[4,4,48,640]{3,2,1,0:T(8,128)(2,1)S(1)}, u32[]{:S(2)}, u32[]{:S(2)}) %collective-permute-start.45) | collective-permute-done | bytes 983072 | tf_op jit(solution)/shard_map/ppermute | solution.py:31
  376.6 5.0 %collective-permute-done.68 = bf16[4,32,640]{2,1,0:T(8,128)(2,1)S(1)} collective-permute-done((bf16[4,32,640]{2,1,0:T(8,128)(2,1)S(1)}, bf16[4,32,640]{2,1,0:T(8,128)(2,1)S(1)}, u32[]{:S(2)}, u32[]{:S(2)}) %collective-permute-start.68) | collective-permute-done | bytes 163872 | tf_op jit(solution)/shard_map/ppermute | solution.py:31
  389.2 5.4 %collective-permute-done.57 = bf16[4,48,640]{2,1,0:T(8,128)(2,1)S(1)} collective-permute-done((bf16[4,48,640]{2,1,0:T(8,128)(2,1)S(1)}, bf16[4,48,640]{2,1,0:T(8,128)(2,1)S(1)}, u32[]{:S(2)}, u32[]{:S(2)}) %collective-permute-start.57) | collective-permute-done | bytes 245792 | tf_op jit(solution)/shard_map/ppermute | solution.py:31
  398.2 6.9 %collective-permute-done.48 = bf16[4,48,640]{2,1,0:T(8,128)(2,1)S(1)} collective-permute-done((bf16[4,48,640]{2,1,0:T(8,128)(2,1)S(1)}, bf16[4,48,640]{2,1,0:T(8,128)(2,1)S(1)}, u32[]{:S(2)}, u32[]{:S(2)}) %collective-permute-start.48) | collective-permute-done | bytes 245792 | tf_op jit(solution)/shard_map/ppermute | solution.py:31
  406.4 5.0 %collective-permute-done.46 = bf16[4,48,640]{2,1,0:T(8,128)(2,1)S(1)} collective-permute-done((bf16[4,48,640]{2,1,0:T(8,128)(2,1)S(1)}, bf16[4,48,640]{2,1,0:T(8,128)(2,1)S(1)}, u32[]{:S(2)}, u32[]{:S(2)}) %collective-permute-start.46) | collective-permute-done | bytes 245792 | tf_op jit(solution)/shard_map/ppermute | solution.py:31
  416.9 6.0 %collective-permute-done.61 = bf16[48,640]{1,0:T(8,128)(2,1)S(1)} collective-permute-done((bf16[48,640]{1,0:T(8,128)(2,1)S(1)}, bf16[48,640]{1,0:T(8,128)(2,1)S(1)}, u32[]{:S(2)}, u32[]{:S(2)}) %collective-permute-start.61) | collective-permute-done | bytes 61472 | tf_op jit(solution)/shard_map/ppermute | solution.py:31
  436.8 19.3 %shard_map.153 = (bf16[2,192,5120]{2,1,0:T(8,128)(2,1)}, bf16[2,192,5120]{2,1,0:T(8,128)(2,1)}, bf16[2,192,5120]{2,1,0:T(8,128)(2,1)}) custom-call(s32[1]{0:T(128)} %bitcast.s.refs_0_, f32[1,5120]{1,0:T(1,128)} %bitcast.270, bf16[4,2,2,4,48,1280]{5,4,3,2,1,0:T(8,128)(2,1)} %bitcast.223, bf16[2,2,4,4,48,1280]{5,4,3,2,1,0:T(8,128)(2,1)} %bitcast.21.cb.xb.refs_3_.refs_6_, ...), custom_call_target="tpu_custom_call" | custom-call | flops 12079595520 | bytes 41943040 | tf_op jit(solution)/shard_map/pallas_call | solution.py:146
  (282 shorter events, 177.1 us)
Async XLA Ops:
  2.5 31.6 %collective-permute-start = (bf16[128,1280]{1,0:T(8,128)(2,1)S(1)}, bf16[128,1280]{1,0:T(8,128)(2,1)S(1)}, u32[]{:S(2)}, u32[]{:S(2)}) collective-permute-start(bf16[128,1280]{1,0:T(8,128)(2,1)S(1)} %constant_dynamic-update-slice_fusion), channel_id=1, source_target_pairs={{0,64},{8,72},{16,80},{24,88},{32,96},{40,104},{48,112},{56,120},{... | collective-permute-start | bytes 983048 | tf_op jit(solution)/shard_map/ppermute | solution.py:184
  6.1 28.0 %collective-permute-start.1 = (bf16[128,1280]{1,0:T(8,128)(2,1)S(1)}, bf16[128,1280]{1,0:T(8,128)(2,1)S(1)}, u32[]{:S(2)}, u32[]{:S(2)}) collective-permute-start(bf16[128,1280]{1,0:T(8,128)(2,1)S(1)} %constant_dynamic-update-slice_fusion), channel_id=1, source_target_pairs={{0,48},{8,56},{16,64},{24,72},{32,80},{40,88},{48,96},{56,104},{64... | collective-permute-start | bytes 983048 | tf_op jit(solution)/shard_map/ppermute | solution.py:184
  10.8 23.5 %collective-permute-start.2 = (bf16[128,1280]{1,0:T(8,128)(2,1)S(1)}, bf16[128,1280]{1,0:T(8,128)(2,1)S(1)}, u32[]{:S(2)}, u32[]{:S(2)}) collective-permute-start(bf16[128,1280]{1,0:T(8,128)(2,1)S(1)} %constant_dynamic-update-slice_fusion), channel_id=1, source_target_pairs={{0,32},{8,40},{16,48},{24,56},{32,64},{40,72},{48,80},{56,88},{64,... | collective-permute-start | bytes 983048 | tf_op jit(solution)/shard_map/ppermute | solution.py:184
  12.4 21.9 %collective-permute-start.3 = (bf16[128,1280]{1,0:T(8,128)(2,1)S(1)}, bf16[128,1280]{1,0:T(8,128)(2,1)S(1)}, u32[]{:S(2)}, u32[]{:S(2)}) collective-permute-start(bf16[128,1280]{1,0:T(8,128)(2,1)S(1)} %constant_dynamic-update-slice_fusion), channel_id=1, source_target_pairs={{0,16},{8,24},{16,32},{24,40},{32,48},{40,56},{48,64},{56,72},{64,... | collective-permute-start | bytes 983048 | tf_op jit(solution)/shard_map/ppermute | solution.py:184
  88.1 27.5 %collective-permute-start.18 = (bf16[4,48,1280]{2,1,0:T(8,128)(2,1)S(1)}, bf16[4,48,1280]{2,1,0:T(8,128)(2,1)S(1)}, u32[]{:S(2)}, u32[]{:S(2)}) collective-permute-start(bf16[4,48,1280]{2,1,0:T(8,128)(2,1)S(1)} %get-tuple-element.66), channel_id=1, source_target_pairs={{0,1},{1,0},{2,3},{3,2},{4,5},{5,4},{6,7},{7,6},{8,9},{9,8},{10,11... | collective-permute-start | bytes 1474568 | tf_op jit(solution)/shard_map/ppermute | solution.py:31
  89.1 51.7 %collective-permute-start.32 = (bf16[4,4,32,1280]{3,2,1,0:T(8,128)(2,1)S(1)}, bf16[4,4,32,1280]{3,2,1,0:T(8,128)(2,1)S(1)}, u32[]{:S(2)}, u32[]{:S(2)}) collective-permute-start(bf16[4,4,32,1280]{3,2,1,0:T(8,128)(2,1)S(1)} %pad_maximum_fusion.2), channel_id=1, source_target_pairs={{0,3},{1,2},{2,1},{3,0},{4,7},{5,6},{6,5},{7,4},{8,11},{9,10},{10,... | collective-permute-start | bytes 3932168 | tf_op jit(solution)/shard_map/ppermute | solution.py:31
  91.5 24.7 %collective-permute-start.19 = (bf16[4,48,1280]{2,1,0:T(8,128)(2,1)S(1)}, bf16[4,48,1280]{2,1,0:T(8,128)(2,1)S(1)}, u32[]{:S(2)}, u32[]{:S(2)}) collective-permute-start(bf16[4,48,1280]{2,1,0:T(8,128)(2,1)S(1)} %get-tuple-element.66), channel_id=1, source_target_pairs={{0,2},{1,3},{2,0},{3,1},{4,6},{5,7},{6,4},{7,5},{8,10},{9,11},{10,... | collective-permute-start | bytes 1474568 | tf_op jit(solution)/shard_map/ppermute | solution.py:31
  97.0 41.7 %collective-permute-start.20 = (bf16[4,48,1280]{2,1,0:T(8,128)(2,1)S(1)}, bf16[4,48,1280]{2,1,0:T(8,128)(2,1)S(1)}, u32[]{:S(2)}, u32[]{:S(2)}) collective-permute-start(bf16[4,48,1280]{2,1,0:T(8,128)(2,1)S(1)} %get-tuple-element.66), channel_id=1, source_target_pairs={{0,3},{1,2},{2,1},{3,0},{4,7},{5,6},{6,5},{7,4},{8,11},{9,10},{10,... | collective-permute-start | bytes 1474568 | tf_op jit(solution)/shard_map/ppermute | solution.py:31
  100.5 41.0 %collective-permute-start.31 = (bf16[4,4,32,1280]{3,2,1,0:T(8,128)(2,1)S(1)}, bf16[4,4,32,1280]{3,2,1,0:T(8,128)(2,1)S(1)}, u32[]{:S(2)}, u32[]{:S(2)}) collective-permute-start(bf16[4,4,32,1280]{3,2,1,0:T(8,128)(2,1)S(1)} %pad_maximum_fusion.2), channel_id=1, source_target_pairs={{0,1},{1,0},{2,3},{3,2},{4,5},{5,4},{6,7},{7,6},{8,9},{9,8},{10,11... | collective-permute-start | bytes 3932168 | tf_op jit(solution)/shard_map/ppermute | solution.py:31
  115.6 50.3 %collective-permute-start.11 = (bf16[4,4,48,1280]{3,2,1,0:T(8,128)(2,1)S(1)}, bf16[4,4,48,1280]{3,2,1,0:T(8,128)(2,1)S(1)}, u32[]{:S(2)}, u32[]{:S(2)}) collective-permute-start(bf16[4,4,48,1280]{3,2,1,0:T(8,128)(2,1)S(1)} %pad_maximum_fusion), channel_id=1, source_target_pairs={{0,16},{1,17},{2,18},{3,19},{4,20},{5,21},{6,22},{7,23},{8,24},{9,... | collective-permute-start | bytes 5898248 | tf_op jit(solution)/shard_map/ppermute | solution.py:31
  116.2 50.3 %collective-permute-start.12 = (bf16[4,4,48,1280]{3,2,1,0:T(8,128)(2,1)S(1)}, bf16[4,4,48,1280]{3,2,1,0:T(8,128)(2,1)S(1)}, u32[]{:S(2)}, u32[]{:S(2)}) collective-permute-start(bf16[4,4,48,1280]{3,2,1,0:T(8,128)(2,1)S(1)} %pad_maximum_fusion), channel_id=1, source_target_pairs={{0,48},{1,49},{2,50},{3,51},{4,52},{5,53},{6,54},{7,55},{8,56},{9,... | collective-permute-start | bytes 5898248 | tf_op jit(solution)/shard_map/ppermute | solution.py:31
  139.7 40.4 %collective-permute-start.21 = (bf16[4,4,48,1280]{3,2,1,0:T(8,128)(2,1)S(1)}, bf16[4,4,48,1280]{3,2,1,0:T(8,128)(2,1)S(1)}, u32[]{:S(2)}, u32[]{:S(2)}) collective-permute-start(bf16[4,4,48,1280]{3,2,1,0:T(8,128)(2,1)S(1)} %pad_maximum_fusion.1), channel_id=1, source_target_pairs={{0,64},{1,65},{2,66},{3,67},{4,68},{5,69},{6,70},{7,71},{8,72},{9,... | collective-permute-start | bytes 5898248 | tf_op jit(solution)/shard_map/ppermute | solution.py:31
  141.5 46.8 %collective-permute-start.22 = (bf16[4,4,48,1280]{3,2,1,0:T(8,128)(2,1)S(1)}, bf16[4,4,48,1280]{3,2,1,0:T(8,128)(2,1)S(1)}, u32[]{:S(2)}, u32[]{:S(2)}) collective-permute-start(bf16[4,4,48,1280]{3,2,1,0:T(8,128)(2,1)S(1)} %pad_maximum_fusion.1), channel_id=1, source_target_pairs={{0,68},{1,69},{2,70},{3,71},{4,64},{5,65},{6,66},{7,67},{8,76},{9,... | collective-permute-start | bytes 5898248 | tf_op jit(solution)/shard_map/ppermute | solution.py:31
  166.0 67.6 %collective-permute-start.35 = (bf16[2,192,5120]{2,1,0:T(8,128)(2,1)S(1)}, bf16[2,192,5120]{2,1,0:T(8,128)(2,1)S(1)}, u32[]{:S(2)}, u32[]{:S(2)}) collective-permute-start(bf16[2,192,5120]{2,1,0:T(8,128)(2,1)S(1)} %copy-done.2), channel_id=1, source_target_pairs={{0,8},{1,9},{2,10},{3,11},{4,12},{5,13},{6,14},{7,15},{8,0},{9,1},... | collective-permute-start | bytes 11796488 | tf_op jit(solution)/shard_map/ppermute | solution.py:31
  166.0 67.6 %collective-permute-start.36 = (bf16[2,192,5120]{2,1,0:T(8,128)(2,1)S(1)}, bf16[2,192,5120]{2,1,0:T(8,128)(2,1)S(1)}, u32[]{:S(2)}, u32[]{:S(2)}) collective-permute-start(bf16[2,192,5120]{2,1,0:T(8,128)(2,1)S(1)} %copy-done.3), channel_id=1, source_target_pairs={{0,8},{1,9},{2,10},{3,11},{4,12},{5,13},{6,14},{7,15},{8,0},{9,1},... | collective-permute-start | bytes 11796488 | tf_op jit(solution)/shard_map/ppermute | solution.py:31
  166.5 69.5 %collective-permute-start.37 = (bf16[2,192,5120]{2,1,0:T(8,128)(2,1)}, bf16[2,192,5120]{2,1,0:T(8,128)(2,1)}, u32[]{:S(2)}, u32[]{:S(2)}) collective-permute-start(bf16[2,192,5120]{2,1,0:T(8,128)(2,1)} %wd0.1), channel_id=1, source_target_pairs={{0,8},{1,9},{2,10},{3,11},{4,12},{5,13},{6,14},{7,15},{8,0},{9,1},... | collective-permute-start | bytes 11796488 | tf_op jit(solution)/shard_map/ppermute | solution.py:31
  188.3 21.8 %collective-permute-start.14 = (bf16[2,4,48,1280]{3,2,1,0:T(8,128)(2,1)S(1)}, bf16[2,4,48,1280]{3,2,1,0:T(8,128)(2,1)S(1)}, u32[]{:S(2)}, u32[]{:S(2)}) collective-permute-start(bf16[2,4,48,1280]{3,2,1,0:T(8,128)(2,1)S(1)} %slice.254), channel_id=1, source_target_pairs={{0,48},{1,49},{2,50},{3,51},{4,52},{5,53},{6,54},{7,55},{8,56},{9,... | collective-permute-start | bytes 2949128 | tf_op jit(solution)/shard_map/ppermute | solution.py:31
  287.7 50.9 %collective-permute-start.62 = (bf16[2,4,32,640]{3,2,1,0:T(8,128)(2,1)S(1)}, bf16[2,4,32,640]{3,2,1,0:T(8,128)(2,1)S(1)}, u32[]{:S(2)}, u32[]{:S(2)}) collective-permute-start(bf16[2,4,32,640]{3,2,1,0:T(8,128)(2,1)S(1)} %get-tuple-element.53), channel_id=1, source_target_pairs={{0,1},{1,0},{2,3},{3,2},{4,5},{5,4},{6,7},{7,6},{8,9},{9,8},{10,11... | collective-permute-start | bytes 983048 | tf_op jit(solution)/shard_map/ppermute | solution.py:31
  289.4 49.9 %collective-permute-start.63 = (bf16[2,4,32,640]{3,2,1,0:T(8,128)(2,1)S(1)}, bf16[2,4,32,640]{3,2,1,0:T(8,128)(2,1)S(1)}, u32[]{:S(2)}, u32[]{:S(2)}) collective-permute-start(bf16[2,4,32,640]{3,2,1,0:T(8,128)(2,1)S(1)} %get-tuple-element.52), channel_id=1, source_target_pairs={{0,3},{1,2},{2,1},{3,0},{4,7},{5,6},{6,5},{7,4},{8,11},{9,10},{10,... | collective-permute-start | bytes 983048 | tf_op jit(solution)/shard_map/ppermute | solution.py:31
  304.8 34.5 %collective-permute-start.52 = (bf16[2,4,48,640]{3,2,1,0:T(8,128)(2,1)S(1)}, bf16[2,4,48,640]{3,2,1,0:T(8,128)(2,1)S(1)}, u32[]{:S(2)}, u32[]{:S(2)}) collective-permute-start(bf16[2,4,48,640]{3,2,1,0:T(8,128)(2,1)S(1)} %get-tuple-element.47), channel_id=1, source_target_pairs={{0,64},{1,65},{2,66},{3,67},{4,68},{5,69},{6,70},{7,71},{8,72},{9,... | collective-permute-start | bytes 1474568 | tf_op jit(solution)/shard_map/ppermute | solution.py:31
  304.9 34.4 %collective-permute-start.53 = (bf16[2,4,48,640]{3,2,1,0:T(8,128)(2,1)S(1)}, bf16[2,4,48,640]{3,2,1,0:T(8,128)(2,1)S(1)}, u32[]{:S(2)}, u32[]{:S(2)}) collective-permute-start(bf16[2,4,48,640]{3,2,1,0:T(8,128)(2,1)S(1)} %get-tuple-element.46), channel_id=1, source_target_pairs={{0,68},{1,69},{2,70},{3,71},{4,64},{5,65},{6,66},{7,67},{8,76},{9,... | collective-permute-start | bytes 1474568 | tf_op jit(solution)/shard_map/ppermute | solution.py:31
  358.0 75.6 %collective-permute-start.72 = (bf16[2,192,5120]{2,1,0:T(8,128)(2,1)S(1)}, bf16[2,192,5120]{2,1,0:T(8,128)(2,1)S(1)}, u32[]{:S(2)}, u32[]{:S(2)}) collective-permute-start(bf16[2,192,5120]{2,1,0:T(8,128)(2,1)S(1)} %copy-done.20), channel_id=1, source_target_pairs={{0,8},{1,9},{2,10},{3,11},{4,12},{5,13},{6,14},{7,15},{8,0},{9,1},... | collective-permute-start | bytes 11796488 | tf_op jit(solution)/shard_map/ppermute | solution.py:31
  358.7 74.9 %collective-permute-start.73 = (bf16[2,192,5120]{2,1,0:T(8,128)(2,1)S(1)}, bf16[2,192,5120]{2,1,0:T(8,128)(2,1)S(1)}, u32[]{:S(2)}, u32[]{:S(2)}) collective-permute-start(bf16[2,192,5120]{2,1,0:T(8,128)(2,1)S(1)} %copy-done.19), channel_id=1, source_target_pairs={{0,8},{1,9},{2,10},{3,11},{4,12},{5,13},{6,14},{7,15},{8,0},{9,1},... | collective-permute-start | bytes 11796488 | tf_op jit(solution)/shard_map/ppermute | solution.py:31
  358.7 74.9 %collective-permute-start.74 = (bf16[2,192,5120]{2,1,0:T(8,128)(2,1)S(1)}, bf16[2,192,5120]{2,1,0:T(8,128)(2,1)}, u32[]{:S(2)}, u32[]{:S(2)}) collective-permute-start(bf16[2,192,5120]{2,1,0:T(8,128)(2,1)S(1)} %copy-done.18), channel_id=1, source_target_pairs={{0,8},{1,9},{2,10},{3,11},{4,12},{5,13},{6,14},{7,15},{8,0},{9,1},... | collective-permute-start | bytes 11796488 | tf_op jit(solution)/shard_map/ppermute | solution.py:31
  (72 other events, 790.2 us)
